TPU v7x, 32 devices: a whole 2x2x4 slice. The times are simulated.
32 devices in a mesh: seq: 8 (over z, x), head: 4 (over y, core).
Axes of the slice: x: 2, y: 2, z: 4, core: 2. Of those that a mesh axis runs over, the one named last changes fastest.
Arguments:
- inputs: float32 [8192, 4096], P('seq', 'head'), may hold values from -6 to 6
- cotangent: float32 [8192, 4096], P('seq', 'head'), may hold values from -1.5 to 1.5
- b_proj: float32 [8192, 128], P('seq'), may hold values from -1.8 to 1.8
- c_proj: float32 [8192, 128], P('seq'), may hold values from -1.8 to 1.8
- decay_rate: float32 [64], P('head'), may hold values from 1e-06 to 0.0001
- level_weight: float32 [8, 64, 8192], P(None, 'head', 'seq'), may hold values from 0 to 2, as said below
- starts: int32 [128], P('seq'), may hold values from 0 to 1, as said below
Outputs:
- grad_x: float32 [8192, 4096], P('seq', 'head')
- grad_b: float32 [8192, 128], P(('seq', 'head'))
- grad_c: float32 [8192, 128], P(('seq', 'head'))
- grad_level: float32 [8, 64, 8192], P(None, 'head', 'seq')
Inputs may be any that keep to these rules, and one draw needn't show every extreme that they name: `starts`: exactly two of the 128 stretches carry 1. `level_weight`: positive.
All inputs are finite; a program needn't handle non-finite values.
Results may differ from a plain program's by a relative error of at most 0.0001.
Values sent between devices are 32-bit elements; how exact they have to be, the bound alone decides.
No kernel may reach another device: no remote copies, remote signals or barrier semaphores. Data moves between devices by JAX's collectives and lax.ppermute only.
A program may use at most 128 MiB of HBM per device.

v0:
```python
import jax
import jax.numpy as jnp
from jax import lax
from jax.sharding import PartitionSpec as P

STRETCH = 64


def from_partner(x, axis, apart):
    return lax.ppermute(x, axis, [(i, i ^ 1 << apart) for i in range(lax.axis_size(axis))])


def local(inputs, cotangent, b_proj, c_proj, decay_rate, level_weight, starts):
    highest = lax.Precision.HIGHEST
    rows_dev = inputs.shape[0]
    head_count = decay_rate.shape[0]
    width = inputs.shape[1] // head_count
    seq_count = lax.axis_size("seq")
    seq_bits = seq_count.bit_length() - 1
    stretch_count = rows_dev // STRETCH
    stretch_bits = stretch_count.bit_length() - 1
    seq_index = lax.axis_index("seq")
    level_count = level_weight.shape[0]
    level_scale = (STRETCH * 2.0 ** jnp.arange(level_count, dtype=jnp.float32)) ** (-0.5)
    level_vals = level_weight * level_scale[:, None, None]
    position = (seq_index * rows_dev + jnp.arange(rows_dev) - seq_count * rows_dev // 2).astype(
        jnp.float32
    )
    decay_query = jnp.exp(-decay_rate[:, None] * position[None, :])
    decay_key = jnp.exp(decay_rate[:, None] * position[None, :])
    open_flag = 1.0 - starts.astype(jnp.float32)
    prefix_open = jnp.cumprod(open_flag)
    suffix_open = jnp.concatenate(
        [jnp.cumprod(open_flag[::-1])[::-1][1:], jnp.ones((1,), jnp.float32)]
    )
    device_clean = prefix_open[stretch_count - 1]
    prefix_rows = jnp.repeat(prefix_open, STRETCH)
    suffix_rows = jnp.repeat(suffix_open, STRETCH)
    x_heads = inputs.reshape(rows_dev, head_count, width)
    cot_heads = cotangent.reshape(rows_dev, head_count, width)
    key_weight = decay_key * suffix_rows[None, :]
    tail_total = jnp.einsum(
        "sn,shp->hnp", b_proj, x_heads * key_weight.T[:, :, None], precision=highest
    )
    query_weight = decay_query * prefix_rows[None, :]
    cross_level = level_vals[stretch_bits + 1 :]
    head_totals = jnp.einsum(
        "tn,kthp->khnp",
        c_proj,
        cot_heads[None] * jnp.transpose(cross_level * query_weight[None], (0, 2, 1))[..., None],
        precision=highest,
    )
    own_clean = device_clean
    before_clean = jnp.float32(1.0)
    after_clean = jnp.float32(1.0)
    carried = head_totals
    fwd_gates = []
    rev_totals = []
    rev_gates = []
    upper_list = []
    for level_bit in range(seq_bits):
        upper_half = (seq_index // 2**level_bit % 2).astype(jnp.float32)
        upper_list.append(upper_half)
        payload = (carried, own_clean)
        received = from_partner((payload[0], payload[1]), "seq", level_bit)
        far_heads = received[0]
        far_clean = received[len(received) - 1]
        rev_totals.append((1.0 - upper_half) * far_heads[0])
        rev_gates.append((1.0 - upper_half) * after_clean)
        fwd_gates.append(upper_half * before_clean)
        carried = upper_half * (far_heads[1:] + far_clean * carried[1:]) + (1.0 - upper_half) * (
            carried[1:] + own_clean * far_heads[1:]
        )
        before_clean = upper_half * far_clean * before_clean + (1.0 - upper_half) * before_clean
        after_clean = (1.0 - upper_half) * far_clean * after_clean + upper_half * after_clean
        own_clean = own_clean * far_clean
    all_tail, all_clean = (
        lax.all_gather(tail_total[None], "seq", axis=0, tiled=True),
        lax.all_gather(device_clean[None], "seq", axis=0, tiled=True),
    )
    zero_count = jnp.cumsum(1.0 - all_clean)
    device_ids = jnp.arange(seq_count)
    weight_rows = []
    for level_bit in range(seq_bits):
        stride = 2**level_bit
        block_base = (seq_index // stride ^ 1) * stride
        block_end = block_base + stride - 1
        end_count = jnp.sum(jnp.where(device_ids == block_end, zero_count, 0.0))
        inside = (
            (device_ids >= block_base) & (device_ids <= block_end) & (end_count - zero_count == 0.0)
        )
        weight_rows.append(jnp.where(inside, 1.0, 0.0) * upper_list[level_bit])
    fwd_state = jnp.einsum("km,mhnp->khnp", jnp.stack(weight_rows), all_tail, precision=highest)
    rev_state = jnp.stack(rev_totals)
    fwd_gate = jnp.stack(fwd_gates)
    rev_gate = jnp.stack(rev_gates)
    query_gate = fwd_gate[:, None, None] * query_weight[None]
    lam_query = cross_level * query_gate
    weighted_cot = cot_heads[None] * jnp.transpose(lam_query, (0, 2, 1))[..., None]
    grad_c_cross = jnp.einsum("kthp,khnp->tn", weighted_cot, fwd_state, precision=highest)
    projected = jnp.einsum("tn,khnp->kthp", c_proj, fwd_state, precision=highest)
    grad_lam_cross = query_gate * jnp.transpose(
        jnp.sum(projected * cot_heads[None], axis=-1), (0, 2, 1)
    )
    rev_combined = jnp.einsum("k,khnp->hnp", rev_gate, rev_state, precision=highest)
    key_rows = key_weight.T[:, :, None]
    grad_x_cross = jnp.einsum("sn,hnp->shp", b_proj, rev_combined, precision=highest) * key_rows
    grad_b_cross = jnp.einsum("shp,hnp->sn", x_heads * key_rows, rev_combined, precision=highest)
    local_stretch = jnp.arange(rows_dev) // STRETCH
    differ = local_stretch[:, None] ^ local_stretch[None, :]
    local_level = jnp.zeros_like(differ)
    for level_bit in range(stretch_bits):
        local_level = local_level + (differ >= 2**level_bit).astype(jnp.int32)
    local_doc = jnp.cumsum(starts)[local_stretch]
    row_ids = jnp.arange(rows_dev)
    valid = (row_ids[:, None] >= row_ids[None, :]) & (local_doc[:, None] == local_doc[None, :])
    scores = jnp.dot(c_proj, b_proj.T, precision=highest)

    def head_step(mixed_sum, pieces):
        x_one, cot_one, query_decay, key_decay, lam_one = pieces
        decayed = jnp.where(valid, query_decay[:, None] * key_decay[None, :], 0.0)
        lam_pair = jnp.zeros((rows_dev, rows_dev), jnp.float32)
        for level in range(stretch_bits + 1):
            lam_pair = jnp.where(local_level == level, lam_one[level][:, None], lam_pair)
        inner = jnp.dot(cot_one, x_one.T, precision=highest)
        kernel = decayed * lam_pair
        weighted = kernel * scores
        plain = decayed * scores * inner
        grad_x_one = jnp.dot(weighted.T, cot_one, precision=highest)
        grad_lam_one = jnp.stack(
            [
                jnp.sum(jnp.where(local_level == level, plain, 0.0), axis=1)
                for level in range(stretch_bits + 1)
            ]
        )
        return (mixed_sum + kernel * inner, (grad_x_one, grad_lam_one))

    pieces = (
        jnp.transpose(x_heads, (1, 0, 2)),
        jnp.transpose(cot_heads, (1, 0, 2)),
        decay_query,
        decay_key,
        jnp.transpose(level_vals[: stretch_bits + 1], (1, 0, 2)),
    )
    mixed_total, (grad_x_local, grad_lam_local) = lax.scan(
        head_step, jnp.zeros((rows_dev, rows_dev), jnp.float32), pieces
    )
    local_c = grad_c_cross + jnp.dot(mixed_total, b_proj, precision=highest)
    local_b = grad_b_cross + jnp.dot(mixed_total.T, c_proj, precision=highest)
    grad_x = (jnp.transpose(grad_x_local, (1, 0, 2)) + grad_x_cross).reshape(
        rows_dev, head_count * width
    )
    grad_level = (
        jnp.concatenate([jnp.transpose(grad_lam_local, (1, 0, 2)), grad_lam_cross], 0)
        * level_scale[:, None, None]
    )
    grad_b, grad_c = (
        lax.psum_scatter(local_b, "head", scatter_dimension=0, tiled=True),
        lax.psum_scatter(local_c, "head", scatter_dimension=0, tiled=True),
    )
    return (grad_x, grad_b, grad_c, grad_level)


def solution(mesh):
    return jax.shard_map(
        local,
        mesh=mesh,
        in_specs=(
            P("seq", "head"),
            P("seq", "head"),
            P("seq", None),
            P("seq", None),
            P("head"),
            P(None, "head", "seq"),
            P("seq"),
        ),
        out_specs=(
            P("seq", "head"),
            P(("seq", "head"), None),
            P(("seq", "head"), None),
            P(None, "head", "seq"),
        ),
        check_vma=False,
    )
```

profile of v0, /device:TPU:0, one launch (start us, length us, event | category | flops | bytes accessed | tf_op | source)
XLA Modules:
  0.0 729.3 jit_solution(16242255150893106869)
XLA Ops:
  7.3 5.4 copy.55
  13.5 6.4 fusion.61
  25.5 21.2 %all-reduce = f32[8]{0:T(128)S(1)} all-reduce(f32[8]{0:T(128)S(1)} %bitcast_dynamic-update-slice_fusion), channel_id=2, replica_groups=mesh['seq'=8,'head'=4] {'seq'}, use_global_device_ids=true, to_apply=%add | all-reduce | flops 8 | bytes 64
  47.0 5.4 copy.54
  62.4 33.9 %all-gather.4.cloned.1.call-done = f32[128,128,64]{1,2,0:T(8,128)} async-done(((f32[16,128,64]{1,2,0:T(8,128)}), f32[128,128,64]{1,2,0:T(8,128)}) %all-gather.4.cloned.1.call-update) | async-done | bytes 4194320 | tf_op jit(solution)/shard_map/all_gather | solution.py:78
  96.4 8.2 %fusion.38 = f32[3,16,128,64]{2,0,3,1:T(4,128)S(1)} fusion(f32[8,16,128,64]{2,3,1,0:T(8,128)} %bitcast.211, f32[1,8]{1,0:T(1,128)S(1)} %get-tuple-element.309, f32[1,8]{1,0:T(1,128)S(1)} %get-tuple-element.310, f32[1,8]{1,0:T(1,128)S(1)} %get-tuple-element.308), kind=kOutput, calls=%fused_computation.60 | convolution fusion | flops 37748784 | bytes 5767264 | tf_op jit(solution)/shard_map/km,mhnp->khnp/dot_general | solution.py:93
  104.6 11.6 %fusion.30 = f32[3,1024,16]{1,2,0:T(8,128)S(1)} fusion(f32[1024,16,64]{0,2,1:T(8,128)S(1)} %bitcast.202, f32[3,16,128,64]{2,0,3,1:T(4,128)S(1)} %fusion.38, f32[1024,128]{1,0:T(8,128)S(1)} %copy-done.5), kind=kOutput, calls=%fused_computation.50 | convolution fusion | flops 4838080512 | bytes 6488064 | tf_op jit(solution)/shard_map/tn,khnp->kthp/dot_general | solution.py:101
  118.0 11.2 %fusion.50 = f32[3,16,128,64]{2,3,1,0:T(8,128)} fusion(f32[3,1024,16]{1,2,0:T(8,128)S(1)} %get-tuple-element.287, f32[1024,16,64]{0,2,1:T(8,128)S(1)} %bitcast.203, f32[1024,128]{1,0:T(8,128)S(1)} %copy-done.5), kind=kOutput, calls=%fused_computation.73 | convolution fusion | flops 4834983936 | bytes 6488064 | tf_op jit(solution)/shard_map/tn,kthp->khnp/dot_general | solution.py:47
  130.8 4.4 compare_select_fusion.1
  135.2 5.4 add_select_fusion
  142.4 5.0 fusion.92
  147.3 17.1 %collective-permute-done.2 = f32[3,16,128,64]{2,3,1,0:T(8,128)} collective-permute-done((f32[3,16,128,64]{2,3,1,0:T(8,128)}, f32[3,16,128,64]{2,3,1,0:T(8,128)}, u32[]{:S(2)}, u32[]{:S(2)}) %collective-permute-start.2) | collective-permute-done | bytes 1572896 | tf_op jit(solution)/shard_map/ppermute | solution.py:10
  164.5 4.1 multiply_add_fusion
  169.6 465.9 %while.16 = (s32[]{:T(128)}, f32[1024,1024]{0,1:T(8,128)}, f32[16,1024,64]{1,2,0:T(8,128)}, f32[16,5,1024]{2,0,1:T(8,128)}, f32[16,1024]{1,0:T(8,128)}, /*index=...) while((s32[]{:T(128)}, f32[1024,1024]{0,1:T(8,128)}, ...), condition=%wide.region_7.8_spmd.clone.clone, body=%wide.region_1.0_spmd.clone.clone.sunk | while | flops 1703930880 | bytes 43289372 | solution.py:145
  171.4 11.7 %multiply_multiply_fusion.4 = (f32[1024,1024]{0,1:T(8,128)S(1)}, f32[1024,1024]{0,1:T(8,128)}) fusion(f32[1024,1024]{0,1:T(8,128)} %get-tuple-element.459, s32[1024]{0:T(1024)S(1)} %get-tuple-element.460, f32[1024]{0:T(1024)S(1)} %bitcast.219, f32[1024]{0:T(1024)S(1)} %bitcast.221, f32[1024]{0:T(1024)S(1)} %bitcast.231, f32[1024]{0:T(1024)S(1)} %bitcast.225, ...), kind=kOutput, calls=%fused_computation.14.clone.1 | convolution fusion | flops 839909376 | bytes 17348096 | tf_op jit(solution)/shard_map/while/body/eval_jaxpr/dot_general | solution.py:125
  183.1 9.5 %fusion.106 = f32[16,1024,64]{1,2,0:T(8,128)} fusion(f32[16,1024,64]{1,2,0:T(8,128)} %get-tuple-element.434, s32[]{:T(128)S(6)} %copy.113, f32[1024,1024]{0,1:T(8,128)S(1)} %copy-done.6, f32[1024]{0:T(1024)S(1)} %bitcast.232, f32[1024]{0:T(1024)S(1)} %bitcast.226, f32[1024]{0:T(1024)S(1)} %bitcast.228, f32[1024]{0:T(1024)S(1)} %bitcast.230, ...), kind=kOutput, calls=%fused_computation.26.clone.1 | convolution fusion | flops 835715072 | bytes 4764672 | tf_op jit(solution)/shard_map/while/body/eval_jaxpr/dot_general | solution.py:129
  192.6 4.1 select_reduce_fusion.6
  200.1 12.1 %multiply_multiply_fusion.4 = (f32[1024,1024]{0,1:T(8,128)S(1)}, f32[1024,1024]{0,1:T(8,128)}) fusion(f32[1024,1024]{0,1:T(8,128)} %get-tuple-element.459, s32[1024]{0:T(1024)S(1)} %get-tuple-element.460, f32[1024]{0:T(1024)S(1)} %bitcast.219, f32[1024]{0:T(1024)S(1)} %bitcast.221, f32[1024]{0:T(1024)S(1)} %bitcast.231, f32[1024]{0:T(1024)S(1)} %bitcast.225, ...), kind=kOutput, calls=%fused_computation.14.clone.1 | convolution fusion | flops 839909376 | bytes 17348096 | tf_op jit(solution)/shard_map/while/body/eval_jaxpr/dot_general | solution.py:125
  212.2 9.5 %fusion.106 = f32[16,1024,64]{1,2,0:T(8,128)} fusion(f32[16,1024,64]{1,2,0:T(8,128)} %get-tuple-element.434, s32[]{:T(128)S(6)} %copy.113, f32[1024,1024]{0,1:T(8,128)S(1)} %copy-done.6, f32[1024]{0:T(1024)S(1)} %bitcast.232, f32[1024]{0:T(1024)S(1)} %bitcast.226, f32[1024]{0:T(1024)S(1)} %bitcast.228, f32[1024]{0:T(1024)S(1)} %bitcast.230, ...), kind=kOutput, calls=%fused_computation.26.clone.1 | convolution fusion | flops 835715072 | bytes 4764672 | tf_op jit(solution)/shard_map/while/body/eval_jaxpr/dot_general | solution.py:129
  221.7 4.1 select_reduce_fusion.6
  229.2 12.1 %multiply_multiply_fusion.4 = (f32[1024,1024]{0,1:T(8,128)S(1)}, f32[1024,1024]{0,1:T(8,128)}) fusion(f32[1024,1024]{0,1:T(8,128)} %get-tuple-element.459, s32[1024]{0:T(1024)S(1)} %get-tuple-element.460, f32[1024]{0:T(1024)S(1)} %bitcast.219, f32[1024]{0:T(1024)S(1)} %bitcast.221, f32[1024]{0:T(1024)S(1)} %bitcast.231, f32[1024]{0:T(1024)S(1)} %bitcast.225, ...), kind=kOutput, calls=%fused_computation.14.clone.1 | convolution fusion | flops 839909376 | bytes 17348096 | tf_op jit(solution)/shard_map/while/body/eval_jaxpr/dot_general | solution.py:125
  241.4 9.5 %fusion.106 = f32[16,1024,64]{1,2,0:T(8,128)} fusion(f32[16,1024,64]{1,2,0:T(8,128)} %get-tuple-element.434, s32[]{:T(128)S(6)} %copy.113, f32[1024,1024]{0,1:T(8,128)S(1)} %copy-done.6, f32[1024]{0:T(1024)S(1)} %bitcast.232, f32[1024]{0:T(1024)S(1)} %bitcast.226, f32[1024]{0:T(1024)S(1)} %bitcast.228, f32[1024]{0:T(1024)S(1)} %bitcast.230, ...), kind=kOutput, calls=%fused_computation.26.clone.1 | convolution fusion | flops 835715072 | bytes 4764672 | tf_op jit(solution)/shard_map/while/body/eval_jaxpr/dot_general | solution.py:129
  250.8 4.1 select_reduce_fusion.6
  258.3 12.1 %multiply_multiply_fusion.4 = (f32[1024,1024]{0,1:T(8,128)S(1)}, f32[1024,1024]{0,1:T(8,128)}) fusion(f32[1024,1024]{0,1:T(8,128)} %get-tuple-element.459, s32[1024]{0:T(1024)S(1)} %get-tuple-element.460, f32[1024]{0:T(1024)S(1)} %bitcast.219, f32[1024]{0:T(1024)S(1)} %bitcast.221, f32[1024]{0:T(1024)S(1)} %bitcast.231, f32[1024]{0:T(1024)S(1)} %bitcast.225, ...), kind=kOutput, calls=%fused_computation.14.clone.1 | convolution fusion | flops 839909376 | bytes 17348096 | tf_op jit(solution)/shard_map/while/body/eval_jaxpr/dot_general | solution.py:125
  270.5 9.5 %fusion.106 = f32[16,1024,64]{1,2,0:T(8,128)} fusion(f32[16,1024,64]{1,2,0:T(8,128)} %get-tuple-element.434, s32[]{:T(128)S(6)} %copy.113, f32[1024,1024]{0,1:T(8,128)S(1)} %copy-done.6, f32[1024]{0:T(1024)S(1)} %bitcast.232, f32[1024]{0:T(1024)S(1)} %bitcast.226, f32[1024]{0:T(1024)S(1)} %bitcast.228, f32[1024]{0:T(1024)S(1)} %bitcast.230, ...), kind=kOutput, calls=%fused_computation.26.clone.1 | convolution fusion | flops 835715072 | bytes 4764672 | tf_op jit(solution)/shard_map/while/body/eval_jaxpr/dot_general | solution.py:129
  279.9 4.1 select_reduce_fusion.6
  287.5 12.1 %multiply_multiply_fusion.4 = (f32[1024,1024]{0,1:T(8,128)S(1)}, f32[1024,1024]{0,1:T(8,128)}) fusion(f32[1024,1024]{0,1:T(8,128)} %get-tuple-element.459, s32[1024]{0:T(1024)S(1)} %get-tuple-element.460, f32[1024]{0:T(1024)S(1)} %bitcast.219, f32[1024]{0:T(1024)S(1)} %bitcast.221, f32[1024]{0:T(1024)S(1)} %bitcast.231, f32[1024]{0:T(1024)S(1)} %bitcast.225, ...), kind=kOutput, calls=%fused_computation.14.clone.1 | convolution fusion | flops 839909376 | bytes 17348096 | tf_op jit(solution)/shard_map/while/body/eval_jaxpr/dot_general | solution.py:125
  299.6 9.5 %fusion.106 = f32[16,1024,64]{1,2,0:T(8,128)} fusion(f32[16,1024,64]{1,2,0:T(8,128)} %get-tuple-element.434, s32[]{:T(128)S(6)} %copy.113, f32[1024,1024]{0,1:T(8,128)S(1)} %copy-done.6, f32[1024]{0:T(1024)S(1)} %bitcast.232, f32[1024]{0:T(1024)S(1)} %bitcast.226, f32[1024]{0:T(1024)S(1)} %bitcast.228, f32[1024]{0:T(1024)S(1)} %bitcast.230, ...), kind=kOutput, calls=%fused_computation.26.clone.1 | convolution fusion | flops 835715072 | bytes 4764672 | tf_op jit(solution)/shard_map/while/body/eval_jaxpr/dot_general | solution.py:129
  316.6 12.1 %multiply_multiply_fusion.4 = (f32[1024,1024]{0,1:T(8,128)S(1)}, f32[1024,1024]{0,1:T(8,128)}) fusion(f32[1024,1024]{0,1:T(8,128)} %get-tuple-element.459, s32[1024]{0:T(1024)S(1)} %get-tuple-element.460, f32[1024]{0:T(1024)S(1)} %bitcast.219, f32[1024]{0:T(1024)S(1)} %bitcast.221, f32[1024]{0:T(1024)S(1)} %bitcast.231, f32[1024]{0:T(1024)S(1)} %bitcast.225, ...), kind=kOutput, calls=%fused_computation.14.clone.1 | convolution fusion | flops 839909376 | bytes 17348096 | tf_op jit(solution)/shard_map/while/body/eval_jaxpr/dot_general | solution.py:125
  328.7 9.5 %fusion.106 = f32[16,1024,64]{1,2,0:T(8,128)} fusion(f32[16,1024,64]{1,2,0:T(8,128)} %get-tuple-element.434, s32[]{:T(128)S(6)} %copy.113, f32[1024,1024]{0,1:T(8,128)S(1)} %copy-done.6, f32[1024]{0:T(1024)S(1)} %bitcast.232, f32[1024]{0:T(1024)S(1)} %bitcast.226, f32[1024]{0:T(1024)S(1)} %bitcast.228, f32[1024]{0:T(1024)S(1)} %bitcast.230, ...), kind=kOutput, calls=%fused_computation.26.clone.1 | convolution fusion | flops 835715072 | bytes 4764672 | tf_op jit(solution)/shard_map/while/body/eval_jaxpr/dot_general | solution.py:129
  338.2 4.1 select_reduce_fusion.6
  345.7 12.1 %multiply_multiply_fusion.4 = (f32[1024,1024]{0,1:T(8,128)S(1)}, f32[1024,1024]{0,1:T(8,128)}) fusion(f32[1024,1024]{0,1:T(8,128)} %get-tuple-element.459, s32[1024]{0:T(1024)S(1)} %get-tuple-element.460, f32[1024]{0:T(1024)S(1)} %bitcast.219, f32[1024]{0:T(1024)S(1)} %bitcast.221, f32[1024]{0:T(1024)S(1)} %bitcast.231, f32[1024]{0:T(1024)S(1)} %bitcast.225, ...), kind=kOutput, calls=%fused_computation.14.clone.1 | convolution fusion | flops 839909376 | bytes 17348096 | tf_op jit(solution)/shard_map/while/body/eval_jaxpr/dot_general | solution.py:125
  357.8 9.5 %fusion.106 = f32[16,1024,64]{1,2,0:T(8,128)} fusion(f32[16,1024,64]{1,2,0:T(8,128)} %get-tuple-element.434, s32[]{:T(128)S(6)} %copy.113, f32[1024,1024]{0,1:T(8,128)S(1)} %copy-done.6, f32[1024]{0:T(1024)S(1)} %bitcast.232, f32[1024]{0:T(1024)S(1)} %bitcast.226, f32[1024]{0:T(1024)S(1)} %bitcast.228, f32[1024]{0:T(1024)S(1)} %bitcast.230, ...), kind=kOutput, calls=%fused_computation.26.clone.1 | convolution fusion | flops 835715072 | bytes 4764672 | tf_op jit(solution)/shard_map/while/body/eval_jaxpr/dot_general | solution.py:129
  374.8 12.1 %multiply_multiply_fusion.4 = (f32[1024,1024]{0,1:T(8,128)S(1)}, f32[1024,1024]{0,1:T(8,128)}) fusion(f32[1024,1024]{0,1:T(8,128)} %get-tuple-element.459, s32[1024]{0:T(1024)S(1)} %get-tuple-element.460, f32[1024]{0:T(1024)S(1)} %bitcast.219, f32[1024]{0:T(1024)S(1)} %bitcast.221, f32[1024]{0:T(1024)S(1)} %bitcast.231, f32[1024]{0:T(1024)S(1)} %bitcast.225, ...), kind=kOutput, calls=%fused_computation.14.clone.1 | convolution fusion | flops 839909376 | bytes 17348096 | tf_op jit(solution)/shard_map/while/body/eval_jaxpr/dot_general | solution.py:125
  386.9 9.5 %fusion.106 = f32[16,1024,64]{1,2,0:T(8,128)} fusion(f32[16,1024,64]{1,2,0:T(8,128)} %get-tuple-element.434, s32[]{:T(128)S(6)} %copy.113, f32[1024,1024]{0,1:T(8,128)S(1)} %copy-done.6, f32[1024]{0:T(1024)S(1)} %bitcast.232, f32[1024]{0:T(1024)S(1)} %bitcast.226, f32[1024]{0:T(1024)S(1)} %bitcast.228, f32[1024]{0:T(1024)S(1)} %bitcast.230, ...), kind=kOutput, calls=%fused_computation.26.clone.1 | convolution fusion | flops 835715072 | bytes 4764672 | tf_op jit(solution)/shard_map/while/body/eval_jaxpr/dot_general | solution.py:129
  403.9 12.1 %multiply_multiply_fusion.4 = (f32[1024,1024]{0,1:T(8,128)S(1)}, f32[1024,1024]{0,1:T(8,128)}) fusion(f32[1024,1024]{0,1:T(8,128)} %get-tuple-element.459, s32[1024]{0:T(1024)S(1)} %get-tuple-element.460, f32[1024]{0:T(1024)S(1)} %bitcast.219, f32[1024]{0:T(1024)S(1)} %bitcast.221, f32[1024]{0:T(1024)S(1)} %bitcast.231, f32[1024]{0:T(1024)S(1)} %bitcast.225, ...), kind=kOutput, calls=%fused_computation.14.clone.1 | convolution fusion | flops 839909376 | bytes 17348096 | tf_op jit(solution)/shard_map/while/body/eval_jaxpr/dot_general | solution.py:125
  416.1 9.5 %fusion.106 = f32[16,1024,64]{1,2,0:T(8,128)} fusion(f32[16,1024,64]{1,2,0:T(8,128)} %get-tuple-element.434, s32[]{:T(128)S(6)} %copy.113, f32[1024,1024]{0,1:T(8,128)S(1)} %copy-done.6, f32[1024]{0:T(1024)S(1)} %bitcast.232, f32[1024]{0:T(1024)S(1)} %bitcast.226, f32[1024]{0:T(1024)S(1)} %bitcast.228, f32[1024]{0:T(1024)S(1)} %bitcast.230, ...), kind=kOutput, calls=%fused_computation.26.clone.1 | convolution fusion | flops 835715072 | bytes 4764672 | tf_op jit(solution)/shard_map/while/body/eval_jaxpr/dot_general | solution.py:129
  433.0 12.1 %multiply_multiply_fusion.4 = (f32[1024,1024]{0,1:T(8,128)S(1)}, f32[1024,1024]{0,1:T(8,128)}) fusion(f32[1024,1024]{0,1:T(8,128)} %get-tuple-element.459, s32[1024]{0:T(1024)S(1)} %get-tuple-element.460, f32[1024]{0:T(1024)S(1)} %bitcast.219, f32[1024]{0:T(1024)S(1)} %bitcast.221, f32[1024]{0:T(1024)S(1)} %bitcast.231, f32[1024]{0:T(1024)S(1)} %bitcast.225, ...), kind=kOutput, calls=%fused_computation.14.clone.1 | convolution fusion | flops 839909376 | bytes 17348096 | tf_op jit(solution)/shard_map/while/body/eval_jaxpr/dot_general | solution.py:125
  445.2 9.5 %fusion.106 = f32[16,1024,64]{1,2,0:T(8,128)} fusion(f32[16,1024,64]{1,2,0:T(8,128)} %get-tuple-element.434, s32[]{:T(128)S(6)} %copy.113, f32[1024,1024]{0,1:T(8,128)S(1)} %copy-done.6, f32[1024]{0:T(1024)S(1)} %bitcast.232, f32[1024]{0:T(1024)S(1)} %bitcast.226, f32[1024]{0:T(1024)S(1)} %bitcast.228, f32[1024]{0:T(1024)S(1)} %bitcast.230, ...), kind=kOutput, calls=%fused_computation.26.clone.1 | convolution fusion | flops 835715072 | bytes 4764672 | tf_op jit(solution)/shard_map/while/body/eval_jaxpr/dot_general | solution.py:129
  462.1 12.1 %multiply_multiply_fusion.4 = (f32[1024,1024]{0,1:T(8,128)S(1)}, f32[1024,1024]{0,1:T(8,128)}) fusion(f32[1024,1024]{0,1:T(8,128)} %get-tuple-element.459, s32[1024]{0:T(1024)S(1)} %get-tuple-element.460, f32[1024]{0:T(1024)S(1)} %bitcast.219, f32[1024]{0:T(1024)S(1)} %bitcast.221, f32[1024]{0:T(1024)S(1)} %bitcast.231, f32[1024]{0:T(1024)S(1)} %bitcast.225, ...), kind=kOutput, calls=%fused_computation.14.clone.1 | convolution fusion | flops 839909376 | bytes 17348096 | tf_op jit(solution)/shard_map/while/body/eval_jaxpr/dot_general | solution.py:125
  474.3 9.5 %fusion.106 = f32[16,1024,64]{1,2,0:T(8,128)} fusion(f32[16,1024,64]{1,2,0:T(8,128)} %get-tuple-element.434, s32[]{:T(128)S(6)} %copy.113, f32[1024,1024]{0,1:T(8,128)S(1)} %copy-done.6, f32[1024]{0:T(1024)S(1)} %bitcast.232, f32[1024]{0:T(1024)S(1)} %bitcast.226, f32[1024]{0:T(1024)S(1)} %bitcast.228, f32[1024]{0:T(1024)S(1)} %bitcast.230, ...), kind=kOutput, calls=%fused_computation.26.clone.1 | convolution fusion | flops 835715072 | bytes 4764672 | tf_op jit(solution)/shard_map/while/body/eval_jaxpr/dot_general | solution.py:129
  483.7 4.1 select_reduce_fusion.6
  491.2 12.1 %multiply_multiply_fusion.4 = (f32[1024,1024]{0,1:T(8,128)S(1)}, f32[1024,1024]{0,1:T(8,128)}) fusion(f32[1024,1024]{0,1:T(8,128)} %get-tuple-element.459, s32[1024]{0:T(1024)S(1)} %get-tuple-element.460, f32[1024]{0:T(1024)S(1)} %bitcast.219, f32[1024]{0:T(1024)S(1)} %bitcast.221, f32[1024]{0:T(1024)S(1)} %bitcast.231, f32[1024]{0:T(1024)S(1)} %bitcast.225, ...), kind=kOutput, calls=%fused_computation.14.clone.1 | convolution fusion | flops 839909376 | bytes 17348096 | tf_op jit(solution)/shard_map/while/body/eval_jaxpr/dot_general | solution.py:125
  503.4 9.4 %fusion.106 = f32[16,1024,64]{1,2,0:T(8,128)} fusion(f32[16,1024,64]{1,2,0:T(8,128)} %get-tuple-element.434, s32[]{:T(128)S(6)} %copy.113, f32[1024,1024]{0,1:T(8,128)S(1)} %copy-done.6, f32[1024]{0:T(1024)S(1)} %bitcast.232, f32[1024]{0:T(1024)S(1)} %bitcast.226, f32[1024]{0:T(1024)S(1)} %bitcast.228, f32[1024]{0:T(1024)S(1)} %bitcast.230, ...), kind=kOutput, calls=%fused_computation.26.clone.1 | convolution fusion | flops 835715072 | bytes 4764672 | tf_op jit(solution)/shard_map/while/body/eval_jaxpr/dot_general | solution.py:129
  512.8 4.1 select_reduce_fusion.6
  520.3 12.1 %multiply_multiply_fusion.4 = (f32[1024,1024]{0,1:T(8,128)S(1)}, f32[1024,1024]{0,1:T(8,128)}) fusion(f32[1024,1024]{0,1:T(8,128)} %get-tuple-element.459, s32[1024]{0:T(1024)S(1)} %get-tuple-element.460, f32[1024]{0:T(1024)S(1)} %bitcast.219, f32[1024]{0:T(1024)S(1)} %bitcast.221, f32[1024]{0:T(1024)S(1)} %bitcast.231, f32[1024]{0:T(1024)S(1)} %bitcast.225, ...), kind=kOutput, calls=%fused_computation.14.clone.1 | convolution fusion | flops 839909376 | bytes 17348096 | tf_op jit(solution)/shard_map/while/body/eval_jaxpr/dot_general | solution.py:125
  532.5 9.4 %fusion.106 = f32[16,1024,64]{1,2,0:T(8,128)} fusion(f32[16,1024,64]{1,2,0:T(8,128)} %get-tuple-element.434, s32[]{:T(128)S(6)} %copy.113, f32[1024,1024]{0,1:T(8,128)S(1)} %copy-done.6, f32[1024]{0:T(1024)S(1)} %bitcast.232, f32[1024]{0:T(1024)S(1)} %bitcast.226, f32[1024]{0:T(1024)S(1)} %bitcast.228, f32[1024]{0:T(1024)S(1)} %bitcast.230, ...), kind=kOutput, calls=%fused_computation.26.clone.1 | convolution fusion | flops 835715072 | bytes 4764672 | tf_op jit(solution)/shard_map/while/body/eval_jaxpr/dot_general | solution.py:129
  549.4 12.1 %multiply_multiply_fusion.4 = (f32[1024,1024]{0,1:T(8,128)S(1)}, f32[1024,1024]{0,1:T(8,128)}) fusion(f32[1024,1024]{0,1:T(8,128)} %get-tuple-element.459, s32[1024]{0:T(1024)S(1)} %get-tuple-element.460, f32[1024]{0:T(1024)S(1)} %bitcast.219, f32[1024]{0:T(1024)S(1)} %bitcast.221, f32[1024]{0:T(1024)S(1)} %bitcast.231, f32[1024]{0:T(1024)S(1)} %bitcast.225, ...), kind=kOutput, calls=%fused_computation.14.clone.1 | convolution fusion | flops 839909376 | bytes 17348096 | tf_op jit(solution)/shard_map/while/body/eval_jaxpr/dot_general | solution.py:125
  561.6 9.4 %fusion.106 = f32[16,1024,64]{1,2,0:T(8,128)} fusion(f32[16,1024,64]{1,2,0:T(8,128)} %get-tuple-element.434, s32[]{:T(128)S(6)} %copy.113, f32[1024,1024]{0,1:T(8,128)S(1)} %copy-done.6, f32[1024]{0:T(1024)S(1)} %bitcast.232, f32[1024]{0:T(1024)S(1)} %bitcast.226, f32[1024]{0:T(1024)S(1)} %bitcast.228, f32[1024]{0:T(1024)S(1)} %bitcast.230, ...), kind=kOutput, calls=%fused_computation.26.clone.1 | convolution fusion | flops 835715072 | bytes 4764672 | tf_op jit(solution)/shard_map/while/body/eval_jaxpr/dot_general | solution.py:129
  578.5 12.1 %multiply_multiply_fusion.4 = (f32[1024,1024]{0,1:T(8,128)S(1)}, f32[1024,1024]{0,1:T(8,128)}) fusion(f32[1024,1024]{0,1:T(8,128)} %get-tuple-element.459, s32[1024]{0:T(1024)S(1)} %get-tuple-element.460, f32[1024]{0:T(1024)S(1)} %bitcast.219, f32[1024]{0:T(1024)S(1)} %bitcast.221, f32[1024]{0:T(1024)S(1)} %bitcast.231, f32[1024]{0:T(1024)S(1)} %bitcast.225, ...), kind=kOutput, calls=%fused_computation.14.clone.1 | convolution fusion | flops 839909376 | bytes 17348096 | tf_op jit(solution)/shard_map/while/body/eval_jaxpr/dot_general | solution.py:125
  590.7 9.4 %fusion.106 = f32[16,1024,64]{1,2,0:T(8,128)} fusion(f32[16,1024,64]{1,2,0:T(8,128)} %get-tuple-element.434, s32[]{:T(128)S(6)} %copy.113, f32[1024,1024]{0,1:T(8,128)S(1)} %copy-done.6, f32[1024]{0:T(1024)S(1)} %bitcast.232, f32[1024]{0:T(1024)S(1)} %bitcast.226, f32[1024]{0:T(1024)S(1)} %bitcast.228, f32[1024]{0:T(1024)S(1)} %bitcast.230, ...), kind=kOutput, calls=%fused_computation.26.clone.1 | convolution fusion | flops 835715072 | bytes 4764672 | tf_op jit(solution)/shard_map/while/body/eval_jaxpr/dot_general | solution.py:129
  600.1 4.1 select_reduce_fusion.6
  607.6 12.1 %multiply_multiply_fusion.4 = (f32[1024,1024]{0,1:T(8,128)S(1)}, f32[1024,1024]{0,1:T(8,128)}) fusion(f32[1024,1024]{0,1:T(8,128)} %get-tuple-element.459, s32[1024]{0:T(1024)S(1)} %get-tuple-element.460, f32[1024]{0:T(1024)S(1)} %bitcast.219, f32[1024]{0:T(1024)S(1)} %bitcast.221, f32[1024]{0:T(1024)S(1)} %bitcast.231, f32[1024]{0:T(1024)S(1)} %bitcast.225, ...), kind=kOutput, calls=%fused_computation.14.clone.1 | convolution fusion | flops 839909376 | bytes 17348096 | tf_op jit(solution)/shard_map/while/body/eval_jaxpr/dot_general | solution.py:125
  619.7 9.5 %fusion.106 = f32[16,1024,64]{1,2,0:T(8,128)} fusion(f32[16,1024,64]{1,2,0:T(8,128)} %get-tuple-element.434, s32[]{:T(128)S(6)} %copy.113, f32[1024,1024]{0,1:T(8,128)S(1)} %copy-done.6, f32[1024]{0:T(1024)S(1)} %bitcast.232, f32[1024]{0:T(1024)S(1)} %bitcast.226, f32[1024]{0:T(1024)S(1)} %bitcast.228, f32[1024]{0:T(1024)S(1)} %bitcast.230, ...), kind=kOutput, calls=%fused_computation.26.clone.1 | convolution fusion | flops 835715072 | bytes 4764672 | tf_op jit(solution)/shard_map/while/body/eval_jaxpr/dot_general | solution.py:129
  629.2 4.1 select_reduce_fusion.6
  636.8 22.2 %fusion.53 = f32[1024,128]{1,0:T(8,128)S(1)} fusion(f32[3,16,128,64]{2,0,3,1:T(4,128)S(1)} %fusion.38, f32[3,1024,16]{1,2,0:T(8,128)} %get-tuple-element.286, f32[1024,16,64]{0,2,1:T(8,128)} %bitcast.204), kind=kOutput, calls=%fused_computation.74 | convolution fusion | flops 4834983936 | bytes 6488064 | tf_op jit(solution)/shard_map/kthp,khnp->tn/dot_general | solution.py:100
  663.7 7.7 %convolution_add_fusion = f32[1024,128]{1,0:T(8,128)} fusion(f32[1024,128]{1,0:T(8,128)S(1)} %fusion.53, f32[1024,1024]{0,1:T(8,128)S(1)} %copy-done.3, f32[1024,128]{1,0:T(8,128)S(1)} %copy-done), kind=kOutput, calls=%fused_computation.75 | convolution fusion | flops 1610743808 | bytes 5767168 | tf_op jit(solution)/shard_map/dot_general | solution.py:148
  672.7 12.9 %collective-permute-done.4 = f32[1,16,128,64]{2,3,1,0:T(8,128)S(1)} collective-permute-done((f32[1,16,128,64]{2,3,1,0:T(8,128)S(1)}, f32[1,16,128,64]{2,3,1,0:T(8,128)S(1)}, u32[]{:S(2)}, u32[]{:S(2)}) %collective-permute-start.4) | collective-permute-done | bytes 524320 | tf_op jit(solution)/shard_map/ppermute | solution.py:10
  685.9 4.5 fusion.44
  690.4 6.7 fusion.58
  697.1 4.3 convolution_add_fusion.1
  702.3 6.7 fusion.37
  709.0 5.4 copy.68
  714.4 8.2 %reduce-scatter.3.cloned.1.call-done = f32[256,128]{1,0:T(8,128)} async-done(((f32[1024,128]{1,0:T(8,128)}), f32[256,128]{1,0:T(8,128)}) %reduce-scatter.3.cloned.1.call-update) | async-done | bytes 131088 | tf_op jit(solution)/shard_map/reduce_scatter | solution.py:158
  (209 shorter events, 109.7 us)
Async XLA Ops:
  7.2 6.3 copy-start
  7.2 89.2 %all-gather.4.cloned.1.call-start = ((), (), s32[]{:S(2)}) async-start(), calls=%async_computation.4 | async-start | bytes 4718592 | tf_op jit(solution)/shard_map/all_gather | solution.py:78
  7.2 5.4 copy-start.10
  7.3 6.1 copy-start.9
  12.7 7.9 %copy-start.11 = (u32[32]{0:T(128)S(1)}, u32[32]{0:T(128)}, u32[]{:S(2)}) copy-start(u32[32]{0:T(128)} %constant.177) | copy-start | bytes 388
  19.9 694.5 %reduce-scatter.5.cloned.1.call-start = ((), (), s32[]{:S(2)}) async-start(), calls=%async_computation.3 | async-start | bytes 655360 | tf_op jit(solution)/shard_map/reduce_scatter | solution.py:159
  22.5 34.3 %collective-permute-start = (f32[]{:T(128)}, f32[]{:T(128)}, u32[]{:S(2)}, u32[]{:S(2)}) collective-permute-start(f32[]{:T(128)} %bitcast.26), channel_id=1, source_target_pairs={{0,4},{4,0},{8,12},{12,8},{16,20},{20,16},{24,28},{28,24},{1,5},{5... | collective-permute-start | bytes 20 | tf_op jit(solution)/shard_map/ppermute | solution.py:10
  47.0 8.9 %copy-start.7 = (f32[8,16,1024]{2,1,0:T(8,128)S(1)}, f32[8,16,1024]{2,1,0:T(8,128)}, u32[]{:S(2)}) copy-start(f32[8,16,1024]{2,1,0:T(8,128)} %param.14) | copy-start | bytes 1572868
  52.4 52.2 %copy-start.5 = (f32[1024,128]{1,0:T(8,128)S(1)}, f32[1024,128]{1,0:T(8,128)}, u32[]{:S(2)}) copy-start(f32[1024,128]{1,0:T(8,128)} %param.12) | copy-start | bytes 1572868
  58.1 3.6 collective-permute-start.1
  96.3 8.3 %copy-start.1 = (f32[1024,1024]{0,1:T(8,128)S(1)}, f32[1024,1024]{0,1:T(8,128)}, u32[]{:S(2)}) copy-start(f32[1024,1024]{0,1:T(8,128)} %copy.54) | copy-start | bytes 12582916
  129.2 35.3 %collective-permute-start.2 = (f32[3,16,128,64]{2,3,1,0:T(8,128)}, f32[3,16,128,64]{2,3,1,0:T(8,128)}, u32[]{:S(2)}, u32[]{:S(2)}) collective-permute-start(f32[3,16,128,64]{2,3,1,0:T(8,128)} %fusion.50), channel_id=1, source_target_pairs={{0,4},{4,0},{8,12},{12,8},{16,20},{20,16},{24,28},{28,24},{1,5},{5... | collective-permute-start | bytes 4718600 | tf_op jit(solution)/shard_map/ppermute | solution.py:10
  168.6 490.4 %collective-permute-start.3 = (f32[2,16,128,64]{2,3,1,0:T(8,128)}, f32[2,16,128,64]{2,3,1,0:T(8,128)}, u32[]{:S(2)}, u32[]{:S(2)}) collective-permute-start(f32[2,16,128,64]{2,3,1,0:T(8,128)} %multiply_add_fusion), channel_id=1, source_target_pairs={{0,8},{4,12},{8,0},{12,4},{16,24},{20,28},{24,16},{28,20},{1,9},{5... | collective-permute-start | bytes 3145736 | tf_op jit(solution)/shard_map/ppermute | solution.py:10
  171.4 11.7 %copy-start.6 = (f32[1024,1024]{0,1:T(8,128)S(1)}, f32[1024,1024]{0,1:T(8,128)}, u32[]{:S(2)}) copy-start(f32[1024,1024]{0,1:T(8,128)} %get-tuple-element.459) | copy-start | bytes 12582916 | tf_op jit(solution)/shard_map/while
  200.1 12.1 %copy-start.6 = (f32[1024,1024]{0,1:T(8,128)S(1)}, f32[1024,1024]{0,1:T(8,128)}, u32[]{:S(2)}) copy-start(f32[1024,1024]{0,1:T(8,128)} %get-tuple-element.459) | copy-start | bytes 12582916 | tf_op jit(solution)/shard_map/while
  229.2 12.1 %copy-start.6 = (f32[1024,1024]{0,1:T(8,128)S(1)}, f32[1024,1024]{0,1:T(8,128)}, u32[]{:S(2)}) copy-start(f32[1024,1024]{0,1:T(8,128)} %get-tuple-element.459) | copy-start | bytes 12582916 | tf_op jit(solution)/shard_map/while
  258.3 12.1 %copy-start.6 = (f32[1024,1024]{0,1:T(8,128)S(1)}, f32[1024,1024]{0,1:T(8,128)}, u32[]{:S(2)}) copy-start(f32[1024,1024]{0,1:T(8,128)} %get-tuple-element.459) | copy-start | bytes 12582916 | tf_op jit(solution)/shard_map/while
  287.5 12.1 %copy-start.6 = (f32[1024,1024]{0,1:T(8,128)S(1)}, f32[1024,1024]{0,1:T(8,128)}, u32[]{:S(2)}) copy-start(f32[1024,1024]{0,1:T(8,128)} %get-tuple-element.459) | copy-start | bytes 12582916 | tf_op jit(solution)/shard_map/while
  316.6 12.1 %copy-start.6 = (f32[1024,1024]{0,1:T(8,128)S(1)}, f32[1024,1024]{0,1:T(8,128)}, u32[]{:S(2)}) copy-start(f32[1024,1024]{0,1:T(8,128)} %get-tuple-element.459) | copy-start | bytes 12582916 | tf_op jit(solution)/shard_map/while
  345.7 12.1 %copy-start.6 = (f32[1024,1024]{0,1:T(8,128)S(1)}, f32[1024,1024]{0,1:T(8,128)}, u32[]{:S(2)}) copy-start(f32[1024,1024]{0,1:T(8,128)} %get-tuple-element.459) | copy-start | bytes 12582916 | tf_op jit(solution)/shard_map/while
  374.8 12.1 %copy-start.6 = (f32[1024,1024]{0,1:T(8,128)S(1)}, f32[1024,1024]{0,1:T(8,128)}, u32[]{:S(2)}) copy-start(f32[1024,1024]{0,1:T(8,128)} %get-tuple-element.459) | copy-start | bytes 12582916 | tf_op jit(solution)/shard_map/while
  403.9 12.1 %copy-start.6 = (f32[1024,1024]{0,1:T(8,128)S(1)}, f32[1024,1024]{0,1:T(8,128)}, u32[]{:S(2)}) copy-start(f32[1024,1024]{0,1:T(8,128)} %get-tuple-element.459) | copy-start | bytes 12582916 | tf_op jit(solution)/shard_map/while
  433.0 12.1 %copy-start.6 = (f32[1024,1024]{0,1:T(8,128)S(1)}, f32[1024,1024]{0,1:T(8,128)}, u32[]{:S(2)}) copy-start(f32[1024,1024]{0,1:T(8,128)} %get-tuple-element.459) | copy-start | bytes 12582916 | tf_op jit(solution)/shard_map/while
  462.1 12.1 %copy-start.6 = (f32[1024,1024]{0,1:T(8,128)S(1)}, f32[1024,1024]{0,1:T(8,128)}, u32[]{:S(2)}) copy-start(f32[1024,1024]{0,1:T(8,128)} %get-tuple-element.459) | copy-start | bytes 12582916 | tf_op jit(solution)/shard_map/while
  491.2 12.1 %copy-start.6 = (f32[1024,1024]{0,1:T(8,128)S(1)}, f32[1024,1024]{0,1:T(8,128)}, u32[]{:S(2)}) copy-start(f32[1024,1024]{0,1:T(8,128)} %get-tuple-element.459) | copy-start | bytes 12582916 | tf_op jit(solution)/shard_map/while
  520.3 12.1 %copy-start.6 = (f32[1024,1024]{0,1:T(8,128)S(1)}, f32[1024,1024]{0,1:T(8,128)}, u32[]{:S(2)}) copy-start(f32[1024,1024]{0,1:T(8,128)} %get-tuple-element.459) | copy-start | bytes 12582916 | tf_op jit(solution)/shard_map/while
  549.4 12.1 %copy-start.6 = (f32[1024,1024]{0,1:T(8,128)S(1)}, f32[1024,1024]{0,1:T(8,128)}, u32[]{:S(2)}) copy-start(f32[1024,1024]{0,1:T(8,128)} %get-tuple-element.459) | copy-start | bytes 12582916 | tf_op jit(solution)/shard_map/while
  578.5 12.1 %copy-start.6 = (f32[1024,1024]{0,1:T(8,128)S(1)}, f32[1024,1024]{0,1:T(8,128)}, u32[]{:S(2)}) copy-start(f32[1024,1024]{0,1:T(8,128)} %get-tuple-element.459) | copy-start | bytes 12582916 | tf_op jit(solution)/shard_map/while
  607.6 12.1 %copy-start.6 = (f32[1024,1024]{0,1:T(8,128)S(1)}, f32[1024,1024]{0,1:T(8,128)}, u32[]{:S(2)}) copy-start(f32[1024,1024]{0,1:T(8,128)} %get-tuple-element.459) | copy-start | bytes 12582916 | tf_op jit(solution)/shard_map/while
  636.8 26.9 %copy-start.3 = (f32[1024,1024]{0,1:T(8,128)S(1)}, f32[1024,1024]{0,1:T(8,128)}, u32[]{:S(2)}) copy-start(f32[1024,1024]{0,1:T(8,128)} %get-tuple-element.96) | copy-start | bytes 12582916
  661.2 24.5 %collective-permute-start.4 = (f32[1,16,128,64]{2,3,1,0:T(8,128)S(1)}, f32[1,16,128,64]{2,3,1,0:T(8,128)S(1)}, u32[]{:S(2)}, u32[]{:S(2)}) collective-permute-start(f32[1,16,128,64]{2,3,1,0:T(8,128)S(1)} %get-tuple-element.285), channel_id=1, source_target_pairs={{0,16},{4,20},{8,24},{12,28},{16,0},{20,4},{24,8},{28,12},{1,17},{... | collective-permute-start | bytes 1572872 | tf_op jit(solution)/shard_map/ppermute | solution.py:10
  671.4 51.1 %reduce-scatter.3.cloned.1.call-start = ((), (), s32[]{:S(2)}) async-start(), calls=%async_computation.2 | async-start | bytes 655360 | tf_op jit(solution)/shard_map/reduce_scatter | solution.py:158
  671.5 18.9 %copy-start.2 = (f32[16,1024,64]{1,2,0:T(8,128)S(1)}, f32[16,1024,64]{1,2,0:T(8,128)}, u32[]{:S(2)}) copy-start(f32[16,1024,64]{1,2,0:T(8,128)} %get-tuple-element.472) | copy-start | bytes 12582916
  685.8 11.3 %copy-start.4 = (f32[1024,1024]{0,1:T(8,128)S(1)}, f32[1024,1024]{0,1:T(8,128)}, u32[]{:S(2)}) copy-start(f32[1024,1024]{0,1:T(8,128)} %get-tuple-element.96) | copy-start | bytes 12582916
  697.1 4.3 copy-start.8
Sparse Core Ops, SparseCore 0:
  20.0 76.3 all-gather.3
  671.5 19.2 reduce-scatter.4
  701.5 20.9 reduce-scatter.2
where the time goes:
time: 737 us; the launch traced here: 729 us
  matrix products  440 us (60%)
  other arithmetic  91.3 us (12%)
  local copies, waits for them, and re-layouts  75.5 us (10%)
  waiting for transfers between devices  73.7 us (10%)
  blocking collectives  21.2 us (3%)
  between operations  18.3 us (2%)
  starting transfers between devices  8.59 us (1%)
    dot_general x16, matrix products, head_step(): inner = jnp.dot(cot_one, x_one.T, precision=highest)  194 us
    dot_general x16, matrix products, head_step(): grad_x_one = jnp.dot(weighted.T, cot_one, precision=highest)  151 us
    reduce_sum x16, other arithmetic, head_step(): jnp.sum(jnp.where(local_level == level, plain, 0.0), axis=1)  66 us
    all_gather x1, waiting for transfers between devices, local(): lax.all_gather(tail_total[None], 'seq', axis=0, tiled=True)  33.9 us
    ppermute x5, waiting for transfers between devices, from_partner(): lax.ppermute(x, axis, [(i, i ^ 1 << apart) for i in range(lax.axis_size(a...  31.6 us
    dynamic_update_slice x32, local copies, waits for them, and re-layouts, local(): lax.scan(head_step, jnp.zeros((rows_dev, rows_dev), jnp.float32), pieces)  26.7 us
    dot_general x1, matrix products, local(): jnp.einsum('kthp,khnp->tn', weighted_cot, fwd_state, precision=highest)  22.2 us
    unnamed x1, blocking collectives  21.2 us
  transfers between devices with their start and end apart: 8, of which 5 were waited for; matrix products, arithmetic and copies ran while one was open for 76% of the time, Pallas kernels for 0%

commit v1 on v0

--- a/solution.py
+++ b/solution.py
@@ -2,6 +2,7 @@
 import jax.numpy as jnp
 from jax import lax
 from jax.sharding import PartitionSpec as P
+from jax.lax import axis_index, axis_size, ppermute
 
 STRETCH = 64
 
@@ -74,8 +75,20 @@
         before_clean = upper_half * far_clean * before_clean + (1.0 - upper_half) * before_clean
         after_clean = (1.0 - upper_half) * far_clean * after_clean + upper_half * after_clean
         own_clean = own_clean * far_clean
+
+    def arrange_tiles(q_in):
+        near, moved = (axis_size("seq"), axis_index("seq"))
+        reached, top = (q_in, 1)
+        while top < near:
+            y = ppermute(reached, "seq", perm=[(b, b ^ top) for b in range(near)])
+            current_arr = jnp.concatenate([reached, y], axis=0)
+            block_next = jnp.concatenate([y, reached], axis=0)
+            reached = jnp.where(moved & top == 0, current_arr, block_next)
+            top = 2 * top
+        return reached
+
     all_tail, all_clean = (
-        lax.all_gather(tail_total[None], "seq", axis=0, tiled=True),
+        arrange_tiles(tail_total[None]),
         lax.all_gather(device_clean[None], "seq", axis=0, tiled=True),
     )
     zero_count = jnp.cumsum(1.0 - all_clean)

time: 737 us -> 813 us (1.10)
  starting transfers between devices: 8.59 us -> 56.5 us
  blocking collectives: 21.2 us -> 54.2 us
    ppermute x5, starting transfers between devices: 8.47 us -> 48.9 us  [from_partner(): lax.ppermute(x, axis, [(i, i ^ 1 << apart) for i in range(lax.axis_size(a...]
    ppermute x0 -> x3, waiting for transfers between devices: none -> 34.6 us  [arrange_tiles(): y = ppermute(reached, 'seq', perm=[(b, b ^ top) for b in range(near)])]
    all_gather x1 -> x0, waiting for transfers between devices: 33.9 us -> none  [local(): lax.all_gather(tail_total[None], 'seq', axis=0, tiled=True)]
    unnamed x1, blocking collectives: 21.2 us -> 54.2 us
    unnamed x28 -> x30, local copies, waits for them, and re-layouts: 18.1 us -> 18.1 us
  transfers between devices with their start and end apart: 8 -> 10, of which waited for: 5 -> 5; matrix products, arithmetic and copies ran while one was open for 76% -> 69% of each run, Pallas kernels for 0% -> 0%
where the time goes in v1:
time: 813 us; the launch traced here: 806 us
  matrix products  436 us (54%)
  other arithmetic  97 us (12%)
  local copies, waits for them, and re-layouts  75.5 us (9%)
  waiting for transfers between devices  67.5 us (8%)
  starting transfers between devices  56.5 us (7%)
  blocking collectives  54.2 us (7%)
  between operations  18.6 us (2%)
    dot_general x16, matrix products, head_step(): inner = jnp.dot(cot_one, x_one.T, precision=highest)  194 us
    dot_general x16, matrix products, head_step(): grad_x_one = jnp.dot(weighted.T, cot_one, precision=highest)  151 us
    reduce_sum x16, other arithmetic, head_step(): jnp.sum(jnp.where(local_level == level, plain, 0.0), axis=1)  66 us
    unnamed x1, blocking collectives  54.2 us
    ppermute x5, starting transfers between devices, from_partner(): lax.ppermute(x, axis, [(i, i ^ 1 << apart) for i in range(lax.axis_size(a...  48.9 us
    ppermute x3, waiting for transfers between devices, arrange_tiles(): y = ppermute(reached, 'seq', perm=[(b, b ^ top) for b in range(near)])  34.6 us
    dynamic_update_slice x32, local copies, waits for them, and re-layouts, local(): lax.scan(head_step, jnp.zeros((rows_dev, rows_dev), jnp.float32), pieces)  26.7 us
    ppermute x5, waiting for transfers between devices, from_partner(): lax.ppermute(x, axis, [(i, i ^ 1 << apart) for i in range(lax.axis_size(a...  24.1 us
  transfers between devices with their start and end apart: 10, of which 5 were waited for; matrix products, arithmetic and copies ran while one was open for 69% of the time, Pallas kernels for 0%

profile of v1, /device:TPU:0, one launch (start us, length us, event | category | flops | bytes accessed | tf_op | source)
XLA Modules:
  0.0 805.9 jit_solution(14678847195894814159)
XLA Ops:
  7.3 5.4 copy.26
  13.4 5.4 fusion.61
  21.9 11.9 %collective-permute-done.5 = f32[1,16,128,64]{2,3,1,0:T(8,128)S(1)} collective-permute-done((f32[1,16,128,64]{2,3,1,0:T(8,128)S(1)}, f32[1,16,128,64]{2,3,1,0:T(8,128)S(1)}, u32[]{:S(2)}, u32[]{:S(2)}) %collective-permute-start.5) | collective-permute-done | bytes 524320 | tf_op jit(solution)/shard_map/ppermute | solution.py:83
  35.8 22.6 %collective-permute-done.6 = f32[2,16,128,64]{2,3,1,0:T(8,128)} collective-permute-done((f32[2,16,128,64]{2,3,1,0:T(8,128)S(1)}, f32[2,16,128,64]{2,3,1,0:T(8,128)}, u32[]{:S(2)}, u32[]{:S(2)}) %collective-permute-start.6) | collective-permute-done | bytes 1048608 | tf_op jit(solution)/shard_map/ppermute | solution.py:83
  67.7 54.2 %all-reduce = f32[8]{0:T(128)S(1)} all-reduce(f32[8]{0:T(128)S(1)} %bitcast_dynamic-update-slice_fusion), channel_id=2, replica_groups=mesh['seq'=8,'head'=4] {'seq'}, use_global_device_ids=true, to_apply=%add | all-reduce | flops 8 | bytes 64
  122.2 5.4 copy.25
  133.3 42.2 %collective-permute-start.1 = (f32[]{:T(128)}, f32[]{:T(128)}, u32[]{:S(2)}, u32[]{:S(2)}) collective-permute-start(f32[]{:T(128)} %mul.366), channel_id=1, source_target_pairs={{0,8},{4,12},{8,0},{12,4},{16,24},{20,28},{24,16},{28,20},{1,9},{5... | collective-permute-start | bytes 20 | tf_op jit(solution)/shard_map/ppermute | solution.py:11
  179.9 5.2 fusion.38
  185.1 11.4 %fusion.30 = f32[3,1024,16]{1,2,0:T(8,128)S(1)} fusion(f32[1024,16,64]{0,2,1:T(8,128)S(1)} %bitcast.203, f32[3,16,128,64]{2,0,3,1:T(4,128)S(1)} %fusion.38, f32[1024,128]{1,0:T(8,128)S(1)} %copy-done.5), kind=kOutput, calls=%fused_computation.50 | convolution fusion | flops 4838080512 | bytes 6488064 | tf_op jit(solution)/shard_map/tn,khnp->kthp/dot_general | solution.py:114
  198.3 11.2 %fusion.50 = f32[3,16,128,64]{2,3,1,0:T(8,128)} fusion(f32[3,1024,16]{1,2,0:T(8,128)S(1)} %get-tuple-element.255, f32[1024,16,64]{0,2,1:T(8,128)S(1)} %bitcast.204, f32[1024,128]{1,0:T(8,128)S(1)} %copy-done.5), kind=kOutput, calls=%fused_computation.75 | convolution fusion | flops 4834983936 | bytes 6488064 | tf_op jit(solution)/shard_map/tn,kthp->khnp/dot_general | solution.py:48
  212.8 4.4 compare_select_fusion.1
  217.2 5.4 add_select_fusion
  224.3 5.0 fusion.92
  229.3 13.5 %collective-permute-done.2 = f32[3,16,128,64]{2,3,1,0:T(8,128)} collective-permute-done((f32[3,16,128,64]{2,3,1,0:T(8,128)}, f32[3,16,128,64]{2,3,1,0:T(8,128)}, u32[]{:S(2)}, u32[]{:S(2)}) %collective-permute-start.2) | collective-permute-done | bytes 1572896 | tf_op jit(solution)/shard_map/ppermute | solution.py:11
  242.8 4.1 multiply_add_fusion
  248.3 465.9 %while.16 = (s32[]{:T(128)}, f32[1024,1024]{0,1:T(8,128)}, f32[16,1024,64]{1,2,0:T(8,128)}, f32[16,5,1024]{2,0,1:T(8,128)}, f32[16,1024]{1,0:T(8,128)}, /*index=...) while((s32[]{:T(128)}, f32[1024,1024]{0,1:T(8,128)}, ...), condition=%wide.region_7.8_spmd.clone.clone, body=%wide.region_1.7_spmd.clone.clone.sunk | while | flops 1703930880 | bytes 43289372 | solution.py:158
  250.4 11.7 %multiply_multiply_fusion.4 = (f32[1024,1024]{0,1:T(8,128)S(1)}, f32[1024,1024]{0,1:T(8,128)}) fusion(f32[1024,1024]{0,1:T(8,128)} %get-tuple-element.427, s32[1024]{0:T(1024)S(1)} %get-tuple-element.428, f32[1024]{0:T(1024)S(1)} %bitcast.219, f32[1024]{0:T(1024)S(1)} %bitcast.221, f32[1024]{0:T(1024)S(1)} %bitcast.231, f32[1024]{0:T(1024)S(1)} %bitcast.225, ...), kind=kOutput, calls=%fused_computation.14.clone.1 | convolution fusion | flops 839909376 | bytes 17348096 | tf_op jit(solution)/shard_map/while/body/eval_jaxpr/dot_general | solution.py:138
  262.1 9.5 %fusion.106 = f32[16,1024,64]{1,2,0:T(8,128)} fusion(f32[16,1024,64]{1,2,0:T(8,128)} %get-tuple-element.402, s32[]{:T(128)S(6)} %copy.84, f32[1024,1024]{0,1:T(8,128)S(1)} %copy-done.7, f32[1024]{0:T(1024)S(1)} %bitcast.232, f32[1024]{0:T(1024)S(1)} %bitcast.226, f32[1024]{0:T(1024)S(1)} %bitcast.228, f32[1024]{0:T(1024)S(1)} %bitcast.230, ...), kind=kOutput, calls=%fused_computation.26.clone.1 | convolution fusion | flops 835715072 | bytes 4764672 | tf_op jit(solution)/shard_map/while/body/eval_jaxpr/dot_general | solution.py:142
  271.6 4.1 select_reduce_fusion.6
  279.1 12.1 %multiply_multiply_fusion.4 = (f32[1024,1024]{0,1:T(8,128)S(1)}, f32[1024,1024]{0,1:T(8,128)}) fusion(f32[1024,1024]{0,1:T(8,128)} %get-tuple-element.427, s32[1024]{0:T(1024)S(1)} %get-tuple-element.428, f32[1024]{0:T(1024)S(1)} %bitcast.219, f32[1024]{0:T(1024)S(1)} %bitcast.221, f32[1024]{0:T(1024)S(1)} %bitcast.231, f32[1024]{0:T(1024)S(1)} %bitcast.225, ...), kind=kOutput, calls=%fused_computation.14.clone.1 | convolution fusion | flops 839909376 | bytes 17348096 | tf_op jit(solution)/shard_map/while/body/eval_jaxpr/dot_general | solution.py:138
  291.2 9.5 %fusion.106 = f32[16,1024,64]{1,2,0:T(8,128)} fusion(f32[16,1024,64]{1,2,0:T(8,128)} %get-tuple-element.402, s32[]{:T(128)S(6)} %copy.84, f32[1024,1024]{0,1:T(8,128)S(1)} %copy-done.7, f32[1024]{0:T(1024)S(1)} %bitcast.232, f32[1024]{0:T(1024)S(1)} %bitcast.226, f32[1024]{0:T(1024)S(1)} %bitcast.228, f32[1024]{0:T(1024)S(1)} %bitcast.230, ...), kind=kOutput, calls=%fused_computation.26.clone.1 | convolution fusion | flops 835715072 | bytes 4764672 | tf_op jit(solution)/shard_map/while/body/eval_jaxpr/dot_general | solution.py:142
  308.2 12.1 %multiply_multiply_fusion.4 = (f32[1024,1024]{0,1:T(8,128)S(1)}, f32[1024,1024]{0,1:T(8,128)}) fusion(f32[1024,1024]{0,1:T(8,128)} %get-tuple-element.427, s32[1024]{0:T(1024)S(1)} %get-tuple-element.428, f32[1024]{0:T(1024)S(1)} %bitcast.219, f32[1024]{0:T(1024)S(1)} %bitcast.221, f32[1024]{0:T(1024)S(1)} %bitcast.231, f32[1024]{0:T(1024)S(1)} %bitcast.225, ...), kind=kOutput, calls=%fused_computation.14.clone.1 | convolution fusion | flops 839909376 | bytes 17348096 | tf_op jit(solution)/shard_map/while/body/eval_jaxpr/dot_general | solution.py:138
  320.4 9.5 %fusion.106 = f32[16,1024,64]{1,2,0:T(8,128)} fusion(f32[16,1024,64]{1,2,0:T(8,128)} %get-tuple-element.402, s32[]{:T(128)S(6)} %copy.84, f32[1024,1024]{0,1:T(8,128)S(1)} %copy-done.7, f32[1024]{0:T(1024)S(1)} %bitcast.232, f32[1024]{0:T(1024)S(1)} %bitcast.226, f32[1024]{0:T(1024)S(1)} %bitcast.228, f32[1024]{0:T(1024)S(1)} %bitcast.230, ...), kind=kOutput, calls=%fused_computation.26.clone.1 | convolution fusion | flops 835715072 | bytes 4764672 | tf_op jit(solution)/shard_map/while/body/eval_jaxpr/dot_general | solution.py:142
  329.8 4.1 select_reduce_fusion.6
  337.3 12.1 %multiply_multiply_fusion.4 = (f32[1024,1024]{0,1:T(8,128)S(1)}, f32[1024,1024]{0,1:T(8,128)}) fusion(f32[1024,1024]{0,1:T(8,128)} %get-tuple-element.427, s32[1024]{0:T(1024)S(1)} %get-tuple-element.428, f32[1024]{0:T(1024)S(1)} %bitcast.219, f32[1024]{0:T(1024)S(1)} %bitcast.221, f32[1024]{0:T(1024)S(1)} %bitcast.231, f32[1024]{0:T(1024)S(1)} %bitcast.225, ...), kind=kOutput, calls=%fused_computation.14.clone.1 | convolution fusion | flops 839909376 | bytes 17348096 | tf_op jit(solution)/shard_map/while/body/eval_jaxpr/dot_general | solution.py:138
  349.5 9.5 %fusion.106 = f32[16,1024,64]{1,2,0:T(8,128)} fusion(f32[16,1024,64]{1,2,0:T(8,128)} %get-tuple-element.402, s32[]{:T(128)S(6)} %copy.84, f32[1024,1024]{0,1:T(8,128)S(1)} %copy-done.7, f32[1024]{0:T(1024)S(1)} %bitcast.232, f32[1024]{0:T(1024)S(1)} %bitcast.226, f32[1024]{0:T(1024)S(1)} %bitcast.228, f32[1024]{0:T(1024)S(1)} %bitcast.230, ...), kind=kOutput, calls=%fused_computation.26.clone.1 | convolution fusion | flops 835715072 | bytes 4764672 | tf_op jit(solution)/shard_map/while/body/eval_jaxpr/dot_general | solution.py:142
  366.5 12.1 %multiply_multiply_fusion.4 = (f32[1024,1024]{0,1:T(8,128)S(1)}, f32[1024,1024]{0,1:T(8,128)}) fusion(f32[1024,1024]{0,1:T(8,128)} %get-tuple-element.427, s32[1024]{0:T(1024)S(1)} %get-tuple-element.428, f32[1024]{0:T(1024)S(1)} %bitcast.219, f32[1024]{0:T(1024)S(1)} %bitcast.221, f32[1024]{0:T(1024)S(1)} %bitcast.231, f32[1024]{0:T(1024)S(1)} %bitcast.225, ...), kind=kOutput, calls=%fused_computation.14.clone.1 | convolution fusion | flops 839909376 | bytes 17348096 | tf_op jit(solution)/shard_map/while/body/eval_jaxpr/dot_general | solution.py:138
  378.6 9.5 %fusion.106 = f32[16,1024,64]{1,2,0:T(8,128)} fusion(f32[16,1024,64]{1,2,0:T(8,128)} %get-tuple-element.402, s32[]{:T(128)S(6)} %copy.84, f32[1024,1024]{0,1:T(8,128)S(1)} %copy-done.7, f32[1024]{0:T(1024)S(1)} %bitcast.232, f32[1024]{0:T(1024)S(1)} %bitcast.226, f32[1024]{0:T(1024)S(1)} %bitcast.228, f32[1024]{0:T(1024)S(1)} %bitcast.230, ...), kind=kOutput, calls=%fused_computation.26.clone.1 | convolution fusion | flops 835715072 | bytes 4764672 | tf_op jit(solution)/shard_map/while/body/eval_jaxpr/dot_general | solution.py:142
  388.1 4.1 select_reduce_fusion.6
  395.6 12.1 %multiply_multiply_fusion.4 = (f32[1024,1024]{0,1:T(8,128)S(1)}, f32[1024,1024]{0,1:T(8,128)}) fusion(f32[1024,1024]{0,1:T(8,128)} %get-tuple-element.427, s32[1024]{0:T(1024)S(1)} %get-tuple-element.428, f32[1024]{0:T(1024)S(1)} %bitcast.219, f32[1024]{0:T(1024)S(1)} %bitcast.221, f32[1024]{0:T(1024)S(1)} %bitcast.231, f32[1024]{0:T(1024)S(1)} %bitcast.225, ...), kind=kOutput, calls=%fused_computation.14.clone.1 | convolution fusion | flops 839909376 | bytes 17348096 | tf_op jit(solution)/shard_map/while/body/eval_jaxpr/dot_general | solution.py:138
  407.7 9.5 %fusion.106 = f32[16,1024,64]{1,2,0:T(8,128)} fusion(f32[16,1024,64]{1,2,0:T(8,128)} %get-tuple-element.402, s32[]{:T(128)S(6)} %copy.84, f32[1024,1024]{0,1:T(8,128)S(1)} %copy-done.7, f32[1024]{0:T(1024)S(1)} %bitcast.232, f32[1024]{0:T(1024)S(1)} %bitcast.226, f32[1024]{0:T(1024)S(1)} %bitcast.228, f32[1024]{0:T(1024)S(1)} %bitcast.230, ...), kind=kOutput, calls=%fused_computation.26.clone.1 | convolution fusion | flops 835715072 | bytes 4764672 | tf_op jit(solution)/shard_map/while/body/eval_jaxpr/dot_general | solution.py:142
  417.2 4.1 select_reduce_fusion.6
  424.7 12.1 %multiply_multiply_fusion.4 = (f32[1024,1024]{0,1:T(8,128)S(1)}, f32[1024,1024]{0,1:T(8,128)}) fusion(f32[1024,1024]{0,1:T(8,128)} %get-tuple-element.427, s32[1024]{0:T(1024)S(1)} %get-tuple-element.428, f32[1024]{0:T(1024)S(1)} %bitcast.219, f32[1024]{0:T(1024)S(1)} %bitcast.221, f32[1024]{0:T(1024)S(1)} %bitcast.231, f32[1024]{0:T(1024)S(1)} %bitcast.225, ...), kind=kOutput, calls=%fused_computation.14.clone.1 | convolution fusion | flops 839909376 | bytes 17348096 | tf_op jit(solution)/shard_map/while/body/eval_jaxpr/dot_general | solution.py:138
  436.8 9.5 %fusion.106 = f32[16,1024,64]{1,2,0:T(8,128)} fusion(f32[16,1024,64]{1,2,0:T(8,128)} %get-tuple-element.402, s32[]{:T(128)S(6)} %copy.84, f32[1024,1024]{0,1:T(8,128)S(1)} %copy-done.7, f32[1024]{0:T(1024)S(1)} %bitcast.232, f32[1024]{0:T(1024)S(1)} %bitcast.226, f32[1024]{0:T(1024)S(1)} %bitcast.228, f32[1024]{0:T(1024)S(1)} %bitcast.230, ...), kind=kOutput, calls=%fused_computation.26.clone.1 | convolution fusion | flops 835715072 | bytes 4764672 | tf_op jit(solution)/shard_map/while/body/eval_jaxpr/dot_general | solution.py:142
  446.3 4.1 select_reduce_fusion.6
  453.8 12.1 %multiply_multiply_fusion.4 = (f32[1024,1024]{0,1:T(8,128)S(1)}, f32[1024,1024]{0,1:T(8,128)}) fusion(f32[1024,1024]{0,1:T(8,128)} %get-tuple-element.427, s32[1024]{0:T(1024)S(1)} %get-tuple-element.428, f32[1024]{0:T(1024)S(1)} %bitcast.219, f32[1024]{0:T(1024)S(1)} %bitcast.221, f32[1024]{0:T(1024)S(1)} %bitcast.231, f32[1024]{0:T(1024)S(1)} %bitcast.225, ...), kind=kOutput, calls=%fused_computation.14.clone.1 | convolution fusion | flops 839909376 | bytes 17348096 | tf_op jit(solution)/shard_map/while/body/eval_jaxpr/dot_general | solution.py:138
  465.9 9.5 %fusion.106 = f32[16,1024,64]{1,2,0:T(8,128)} fusion(f32[16,1024,64]{1,2,0:T(8,128)} %get-tuple-element.402, s32[]{:T(128)S(6)} %copy.84, f32[1024,1024]{0,1:T(8,128)S(1)} %copy-done.7, f32[1024]{0:T(1024)S(1)} %bitcast.232, f32[1024]{0:T(1024)S(1)} %bitcast.226, f32[1024]{0:T(1024)S(1)} %bitcast.228, f32[1024]{0:T(1024)S(1)} %bitcast.230, ...), kind=kOutput, calls=%fused_computation.26.clone.1 | convolution fusion | flops 835715072 | bytes 4764672 | tf_op jit(solution)/shard_map/while/body/eval_jaxpr/dot_general | solution.py:142
  475.4 4.1 select_reduce_fusion.6
  482.9 12.1 %multiply_multiply_fusion.4 = (f32[1024,1024]{0,1:T(8,128)S(1)}, f32[1024,1024]{0,1:T(8,128)}) fusion(f32[1024,1024]{0,1:T(8,128)} %get-tuple-element.427, s32[1024]{0:T(1024)S(1)} %get-tuple-element.428, f32[1024]{0:T(1024)S(1)} %bitcast.219, f32[1024]{0:T(1024)S(1)} %bitcast.221, f32[1024]{0:T(1024)S(1)} %bitcast.231, f32[1024]{0:T(1024)S(1)} %bitcast.225, ...), kind=kOutput, calls=%fused_computation.14.clone.1 | convolution fusion | flops 839909376 | bytes 17348096 | tf_op jit(solution)/shard_map/while/body/eval_jaxpr/dot_general | solution.py:138
  495.0 9.5 %fusion.106 = f32[16,1024,64]{1,2,0:T(8,128)} fusion(f32[16,1024,64]{1,2,0:T(8,128)} %get-tuple-element.402, s32[]{:T(128)S(6)} %copy.84, f32[1024,1024]{0,1:T(8,128)S(1)} %copy-done.7, f32[1024]{0:T(1024)S(1)} %bitcast.232, f32[1024]{0:T(1024)S(1)} %bitcast.226, f32[1024]{0:T(1024)S(1)} %bitcast.228, f32[1024]{0:T(1024)S(1)} %bitcast.230, ...), kind=kOutput, calls=%fused_computation.26.clone.1 | convolution fusion | flops 835715072 | bytes 4764672 | tf_op jit(solution)/shard_map/while/body/eval_jaxpr/dot_general | solution.py:142
  512.0 12.1 %multiply_multiply_fusion.4 = (f32[1024,1024]{0,1:T(8,128)S(1)}, f32[1024,1024]{0,1:T(8,128)}) fusion(f32[1024,1024]{0,1:T(8,128)} %get-tuple-element.427, s32[1024]{0:T(1024)S(1)} %get-tuple-element.428, f32[1024]{0:T(1024)S(1)} %bitcast.219, f32[1024]{0:T(1024)S(1)} %bitcast.221, f32[1024]{0:T(1024)S(1)} %bitcast.231, f32[1024]{0:T(1024)S(1)} %bitcast.225, ...), kind=kOutput, calls=%fused_computation.14.clone.1 | convolution fusion | flops 839909376 | bytes 17348096 | tf_op jit(solution)/shard_map/while/body/eval_jaxpr/dot_general | solution.py:138
  524.2 9.5 %fusion.106 = f32[16,1024,64]{1,2,0:T(8,128)} fusion(f32[16,1024,64]{1,2,0:T(8,128)} %get-tuple-element.402, s32[]{:T(128)S(6)} %copy.84, f32[1024,1024]{0,1:T(8,128)S(1)} %copy-done.7, f32[1024]{0:T(1024)S(1)} %bitcast.232, f32[1024]{0:T(1024)S(1)} %bitcast.226, f32[1024]{0:T(1024)S(1)} %bitcast.228, f32[1024]{0:T(1024)S(1)} %bitcast.230, ...), kind=kOutput, calls=%fused_computation.26.clone.1 | convolution fusion | flops 835715072 | bytes 4764672 | tf_op jit(solution)/shard_map/while/body/eval_jaxpr/dot_general | solution.py:142
  541.1 12.1 %multiply_multiply_fusion.4 = (f32[1024,1024]{0,1:T(8,128)S(1)}, f32[1024,1024]{0,1:T(8,128)}) fusion(f32[1024,1024]{0,1:T(8,128)} %get-tuple-element.427, s32[1024]{0:T(1024)S(1)} %get-tuple-element.428, f32[1024]{0:T(1024)S(1)} %bitcast.219, f32[1024]{0:T(1024)S(1)} %bitcast.221, f32[1024]{0:T(1024)S(1)} %bitcast.231, f32[1024]{0:T(1024)S(1)} %bitcast.225, ...), kind=kOutput, calls=%fused_computation.14.clone.1 | convolution fusion | flops 839909376 | bytes 17348096 | tf_op jit(solution)/shard_map/while/body/eval_jaxpr/dot_general | solution.py:138
  553.3 9.5 %fusion.106 = f32[16,1024,64]{1,2,0:T(8,128)} fusion(f32[16,1024,64]{1,2,0:T(8,128)} %get-tuple-element.402, s32[]{:T(128)S(6)} %copy.84, f32[1024,1024]{0,1:T(8,128)S(1)} %copy-done.7, f32[1024]{0:T(1024)S(1)} %bitcast.232, f32[1024]{0:T(1024)S(1)} %bitcast.226, f32[1024]{0:T(1024)S(1)} %bitcast.228, f32[1024]{0:T(1024)S(1)} %bitcast.230, ...), kind=kOutput, calls=%fused_computation.26.clone.1 | convolution fusion | flops 835715072 | bytes 4764672 | tf_op jit(solution)/shard_map/while/body/eval_jaxpr/dot_general | solution.py:142
  570.2 12.1 %multiply_multiply_fusion.4 = (f32[1024,1024]{0,1:T(8,128)S(1)}, f32[1024,1024]{0,1:T(8,128)}) fusion(f32[1024,1024]{0,1:T(8,128)} %get-tuple-element.427, s32[1024]{0:T(1024)S(1)} %get-tuple-element.428, f32[1024]{0:T(1024)S(1)} %bitcast.219, f32[1024]{0:T(1024)S(1)} %bitcast.221, f32[1024]{0:T(1024)S(1)} %bitcast.231, f32[1024]{0:T(1024)S(1)} %bitcast.225, ...), kind=kOutput, calls=%fused_computation.14.clone.1 | convolution fusion | flops 839909376 | bytes 17348096 | tf_op jit(solution)/shard_map/while/body/eval_jaxpr/dot_general | solution.py:138
  582.4 9.4 %fusion.106 = f32[16,1024,64]{1,2,0:T(8,128)} fusion(f32[16,1024,64]{1,2,0:T(8,128)} %get-tuple-element.402, s32[]{:T(128)S(6)} %copy.84, f32[1024,1024]{0,1:T(8,128)S(1)} %copy-done.7, f32[1024]{0:T(1024)S(1)} %bitcast.232, f32[1024]{0:T(1024)S(1)} %bitcast.226, f32[1024]{0:T(1024)S(1)} %bitcast.228, f32[1024]{0:T(1024)S(1)} %bitcast.230, ...), kind=kOutput, calls=%fused_computation.26.clone.1 | convolution fusion | flops 835715072 | bytes 4764672 | tf_op jit(solution)/shard_map/while/body/eval_jaxpr/dot_general | solution.py:142
  599.3 12.1 %multiply_multiply_fusion.4 = (f32[1024,1024]{0,1:T(8,128)S(1)}, f32[1024,1024]{0,1:T(8,128)}) fusion(f32[1024,1024]{0,1:T(8,128)} %get-tuple-element.427, s32[1024]{0:T(1024)S(1)} %get-tuple-element.428, f32[1024]{0:T(1024)S(1)} %bitcast.219, f32[1024]{0:T(1024)S(1)} %bitcast.221, f32[1024]{0:T(1024)S(1)} %bitcast.231, f32[1024]{0:T(1024)S(1)} %bitcast.225, ...), kind=kOutput, calls=%fused_computation.14.clone.1 | convolution fusion | flops 839909376 | bytes 17348096 | tf_op jit(solution)/shard_map/while/body/eval_jaxpr/dot_general | solution.py:138
  611.5 9.4 %fusion.106 = f32[16,1024,64]{1,2,0:T(8,128)} fusion(f32[16,1024,64]{1,2,0:T(8,128)} %get-tuple-element.402, s32[]{:T(128)S(6)} %copy.84, f32[1024,1024]{0,1:T(8,128)S(1)} %copy-done.7, f32[1024]{0:T(1024)S(1)} %bitcast.232, f32[1024]{0:T(1024)S(1)} %bitcast.226, f32[1024]{0:T(1024)S(1)} %bitcast.228, f32[1024]{0:T(1024)S(1)} %bitcast.230, ...), kind=kOutput, calls=%fused_computation.26.clone.1 | convolution fusion | flops 835715072 | bytes 4764672 | tf_op jit(solution)/shard_map/while/body/eval_jaxpr/dot_general | solution.py:142
  628.4 12.1 %multiply_multiply_fusion.4 = (f32[1024,1024]{0,1:T(8,128)S(1)}, f32[1024,1024]{0,1:T(8,128)}) fusion(f32[1024,1024]{0,1:T(8,128)} %get-tuple-element.427, s32[1024]{0:T(1024)S(1)} %get-tuple-element.428, f32[1024]{0:T(1024)S(1)} %bitcast.219, f32[1024]{0:T(1024)S(1)} %bitcast.221, f32[1024]{0:T(1024)S(1)} %bitcast.231, f32[1024]{0:T(1024)S(1)} %bitcast.225, ...), kind=kOutput, calls=%fused_computation.14.clone.1 | convolution fusion | flops 839909376 | bytes 17348096 | tf_op jit(solution)/shard_map/while/body/eval_jaxpr/dot_general | solution.py:138
  640.6 9.4 %fusion.106 = f32[16,1024,64]{1,2,0:T(8,128)} fusion(f32[16,1024,64]{1,2,0:T(8,128)} %get-tuple-element.402, s32[]{:T(128)S(6)} %copy.84, f32[1024,1024]{0,1:T(8,128)S(1)} %copy-done.7, f32[1024]{0:T(1024)S(1)} %bitcast.232, f32[1024]{0:T(1024)S(1)} %bitcast.226, f32[1024]{0:T(1024)S(1)} %bitcast.228, f32[1024]{0:T(1024)S(1)} %bitcast.230, ...), kind=kOutput, calls=%fused_computation.26.clone.1 | convolution fusion | flops 835715072 | bytes 4764672 | tf_op jit(solution)/shard_map/while/body/eval_jaxpr/dot_general | solution.py:142
  657.5 12.1 %multiply_multiply_fusion.4 = (f32[1024,1024]{0,1:T(8,128)S(1)}, f32[1024,1024]{0,1:T(8,128)}) fusion(f32[1024,1024]{0,1:T(8,128)} %get-tuple-element.427, s32[1024]{0:T(1024)S(1)} %get-tuple-element.428, f32[1024]{0:T(1024)S(1)} %bitcast.219, f32[1024]{0:T(1024)S(1)} %bitcast.221, f32[1024]{0:T(1024)S(1)} %bitcast.231, f32[1024]{0:T(1024)S(1)} %bitcast.225, ...), kind=kOutput, calls=%fused_computation.14.clone.1 | convolution fusion | flops 839909376 | bytes 17348096 | tf_op jit(solution)/shard_map/while/body/eval_jaxpr/dot_general | solution.py:138
  669.7 9.4 %fusion.106 = f32[16,1024,64]{1,2,0:T(8,128)} fusion(f32[16,1024,64]{1,2,0:T(8,128)} %get-tuple-element.402, s32[]{:T(128)S(6)} %copy.84, f32[1024,1024]{0,1:T(8,128)S(1)} %copy-done.7, f32[1024]{0:T(1024)S(1)} %bitcast.232, f32[1024]{0:T(1024)S(1)} %bitcast.226, f32[1024]{0:T(1024)S(1)} %bitcast.228, f32[1024]{0:T(1024)S(1)} %bitcast.230, ...), kind=kOutput, calls=%fused_computation.26.clone.1 | convolution fusion | flops 835715072 | bytes 4764672 | tf_op jit(solution)/shard_map/while/body/eval_jaxpr/dot_general | solution.py:142
  686.6 12.1 %multiply_multiply_fusion.4 = (f32[1024,1024]{0,1:T(8,128)S(1)}, f32[1024,1024]{0,1:T(8,128)}) fusion(f32[1024,1024]{0,1:T(8,128)} %get-tuple-element.427, s32[1024]{0:T(1024)S(1)} %get-tuple-element.428, f32[1024]{0:T(1024)S(1)} %bitcast.219, f32[1024]{0:T(1024)S(1)} %bitcast.221, f32[1024]{0:T(1024)S(1)} %bitcast.231, f32[1024]{0:T(1024)S(1)} %bitcast.225, ...), kind=kOutput, calls=%fused_computation.14.clone.1 | convolution fusion | flops 839909376 | bytes 17348096 | tf_op jit(solution)/shard_map/while/body/eval_jaxpr/dot_general | solution.py:138
  698.7 9.5 %fusion.106 = f32[16,1024,64]{1,2,0:T(8,128)} fusion(f32[16,1024,64]{1,2,0:T(8,128)} %get-tuple-element.402, s32[]{:T(128)S(6)} %copy.84, f32[1024,1024]{0,1:T(8,128)S(1)} %copy-done.7, f32[1024]{0:T(1024)S(1)} %bitcast.232, f32[1024]{0:T(1024)S(1)} %bitcast.226, f32[1024]{0:T(1024)S(1)} %bitcast.228, f32[1024]{0:T(1024)S(1)} %bitcast.230, ...), kind=kOutput, calls=%fused_computation.26.clone.1 | convolution fusion | flops 835715072 | bytes 4764672 | tf_op jit(solution)/shard_map/while/body/eval_jaxpr/dot_general | solution.py:142
  708.2 4.1 select_reduce_fusion.6
  715.6 22.4 %fusion.53 = f32[1024,128]{1,0:T(8,128)S(1)} fusion(f32[3,16,128,64]{2,0,3,1:T(4,128)S(1)} %fusion.38, f32[3,1024,16]{1,2,0:T(8,128)} %get-tuple-element.254, f32[1024,16,64]{0,2,1:T(8,128)} %bitcast.205), kind=kOutput, calls=%fused_computation.76 | convolution fusion | flops 4834983936 | bytes 6488064 | tf_op jit(solution)/shard_map/kthp,khnp->tn/dot_general | solution.py:113
  741.8 7.7 convolution_add_fusion
  750.8 10.5 %collective-permute-done.4 = f32[1,16,128,64]{2,3,1,0:T(8,128)S(1)} collective-permute-done((f32[1,16,128,64]{2,3,1,0:T(8,128)S(1)}, f32[1,16,128,64]{2,3,1,0:T(8,128)S(1)}, u32[]{:S(2)}, u32[]{:S(2)}) %collective-permute-start.4) | collective-permute-done | bytes 524320 | tf_op jit(solution)/shard_map/ppermute | solution.py:11
  761.6 4.5 fusion.44
  766.0 6.7 fusion.58
  772.8 4.3 convolution_add_fusion.1
  778.0 6.7 fusion.37
  784.7 5.4 copy.39
  790.0 8.8 %reduce-scatter.3.cloned.1.call-done = f32[256,128]{1,0:T(8,128)} async-done(((f32[1024,128]{1,0:T(8,128)}), f32[256,128]{1,0:T(8,128)}) %reduce-scatter.3.cloned.1.call-update) | async-done | bytes 131088 | tf_op jit(solution)/shard_map/reduce_scatter | solution.py:171
  (217 shorter events, 127.8 us)
Async XLA Ops:
  7.2 6.3 copy-start
  7.2 782.9 %reduce-scatter.5.cloned.1.call-start = ((), (), s32[]{:S(2)}) async-start(), calls=%async_computation.3 | async-start | bytes 655360 | tf_op jit(solution)/shard_map/reduce_scatter | solution.py:172
  7.2 5.4 copy-start.11
  7.3 6.1 copy-start.10
  18.9 45.4 %copy-start.12 = (u32[32]{0:T(128)S(1)}, u32[32]{0:T(128)}, u32[]{:S(2)}) copy-start(u32[32]{0:T(128)} %constant.177) | copy-start | bytes 388
  18.9 14.9 %collective-permute-start.5 = (f32[1,16,128,64]{2,3,1,0:T(8,128)S(1)}, f32[1,16,128,64]{2,3,1,0:T(8,128)S(1)}, u32[]{:S(2)}, u32[]{:S(2)}) collective-permute-start(f32[1,16,128,64]{2,3,1,0:T(8,128)S(1)} %fusion.61), channel_id=1, source_target_pairs={{0,4},{4,0},{8,12},{12,8},{16,20},{20,16},{24,28},{28,24},{1,5},{5... | collective-permute-start | bytes 1572872 | tf_op jit(solution)/shard_map/ppermute | solution.py:83
  33.9 1.9 copy-start.6
  33.9 24.5 %collective-permute-start.6 = (f32[2,16,128,64]{2,3,1,0:T(8,128)S(1)}, f32[2,16,128,64]{2,3,1,0:T(8,128)}, u32[]{:S(2)}, u32[]{:S(2)}) collective-permute-start(f32[2,16,128,64]{2,3,1,0:T(8,128)S(1)} %maximum_select_fusion.2), channel_id=1, source_target_pairs={{0,8},{4,12},{8,0},{12,4},{16,24},{20,28},{24,16},{28,20},{1,9},{5... | collective-permute-start | bytes 3145736 | tf_op jit(solution)/shard_map/ppermute | solution.py:83
  61.0 115.9 %collective-permute-start.7 = (f32[4,16,128,64]{2,3,1,0:T(8,128)S(1)}, f32[4,16,128,64]{2,3,1,0:T(8,128)}, u32[]{:S(2)}, u32[]{:S(2)}) collective-permute-start(f32[4,16,128,64]{2,3,1,0:T(8,128)S(1)} %maximum_select_fusion.1), channel_id=1, source_target_pairs={{0,16},{4,20},{8,24},{12,28},{16,0},{20,4},{24,8},{28,12},{1,17},{... | collective-permute-start | bytes 6291464 | tf_op jit(solution)/shard_map/ppermute | solution.py:83
  66.2 65.9 %collective-permute-start = (f32[]{:T(128)}, f32[]{:T(128)}, u32[]{:S(2)}, u32[]{:S(2)}) collective-permute-start(f32[]{:T(128)} %bitcast.26), channel_id=1, source_target_pairs={{0,4},{4,0},{8,12},{12,8},{16,20},{20,16},{24,28},{28,24},{1,5},{5... | collective-permute-start | bytes 20 | tf_op jit(solution)/shard_map/ppermute | solution.py:11
  122.2 8.9 %copy-start.8 = (f32[8,16,1024]{2,1,0:T(8,128)S(1)}, f32[8,16,1024]{2,1,0:T(8,128)}, u32[]{:S(2)}) copy-start(f32[8,16,1024]{2,1,0:T(8,128)} %param.14) | copy-start | bytes 1572868
  133.3 42.9 %collective-permute-start.1 = (f32[]{:T(128)}, f32[]{:T(128)}, u32[]{:S(2)}, u32[]{:S(2)}) collective-permute-start(f32[]{:T(128)} %mul.366), channel_id=1, source_target_pairs={{0,8},{4,12},{8,0},{12,4},{16,24},{20,28},{24,16},{28,20},{1,9},{5... | collective-permute-start | bytes 20 | tf_op jit(solution)/shard_map/ppermute | solution.py:11
  179.9 5.2 copy-start.1
  179.9 5.2 copy-start.5
  209.5 33.3 %collective-permute-start.2 = (f32[3,16,128,64]{2,3,1,0:T(8,128)}, f32[3,16,128,64]{2,3,1,0:T(8,128)}, u32[]{:S(2)}, u32[]{:S(2)}) collective-permute-start(f32[3,16,128,64]{2,3,1,0:T(8,128)} %fusion.50), channel_id=1, source_target_pairs={{0,4},{4,0},{8,12},{12,8},{16,20},{20,16},{24,28},{28,24},{1,5},{5... | collective-permute-start | bytes 4718600 | tf_op jit(solution)/shard_map/ppermute | solution.py:11
  247.0 491.1 %collective-permute-start.3 = (f32[2,16,128,64]{2,3,1,0:T(8,128)}, f32[2,16,128,64]{2,3,1,0:T(8,128)}, u32[]{:S(2)}, u32[]{:S(2)}) collective-permute-start(f32[2,16,128,64]{2,3,1,0:T(8,128)} %multiply_add_fusion), channel_id=1, source_target_pairs={{0,8},{4,12},{8,0},{12,4},{16,24},{20,28},{24,16},{28,20},{1,9},{5... | collective-permute-start | bytes 3145736 | tf_op jit(solution)/shard_map/ppermute | solution.py:11
  250.4 11.7 %copy-start.7 = (f32[1024,1024]{0,1:T(8,128)S(1)}, f32[1024,1024]{0,1:T(8,128)}, u32[]{:S(2)}) copy-start(f32[1024,1024]{0,1:T(8,128)} %get-tuple-element.427) | copy-start | bytes 12582916 | tf_op jit(solution)/shard_map/while
  279.1 12.1 %copy-start.7 = (f32[1024,1024]{0,1:T(8,128)S(1)}, f32[1024,1024]{0,1:T(8,128)}, u32[]{:S(2)}) copy-start(f32[1024,1024]{0,1:T(8,128)} %get-tuple-element.427) | copy-start | bytes 12582916 | tf_op jit(solution)/shard_map/while
  308.2 12.1 %copy-start.7 = (f32[1024,1024]{0,1:T(8,128)S(1)}, f32[1024,1024]{0,1:T(8,128)}, u32[]{:S(2)}) copy-start(f32[1024,1024]{0,1:T(8,128)} %get-tuple-element.427) | copy-start | bytes 12582916 | tf_op jit(solution)/shard_map/while
  337.3 12.1 %copy-start.7 = (f32[1024,1024]{0,1:T(8,128)S(1)}, f32[1024,1024]{0,1:T(8,128)}, u32[]{:S(2)}) copy-start(f32[1024,1024]{0,1:T(8,128)} %get-tuple-element.427) | copy-start | bytes 12582916 | tf_op jit(solution)/shard_map/while
  366.5 12.1 %copy-start.7 = (f32[1024,1024]{0,1:T(8,128)S(1)}, f32[1024,1024]{0,1:T(8,128)}, u32[]{:S(2)}) copy-start(f32[1024,1024]{0,1:T(8,128)} %get-tuple-element.427) | copy-start | bytes 12582916 | tf_op jit(solution)/shard_map/while
  395.6 12.1 %copy-start.7 = (f32[1024,1024]{0,1:T(8,128)S(1)}, f32[1024,1024]{0,1:T(8,128)}, u32[]{:S(2)}) copy-start(f32[1024,1024]{0,1:T(8,128)} %get-tuple-element.427) | copy-start | bytes 12582916 | tf_op jit(solution)/shard_map/while
  424.7 12.1 %copy-start.7 = (f32[1024,1024]{0,1:T(8,128)S(1)}, f32[1024,1024]{0,1:T(8,128)}, u32[]{:S(2)}) copy-start(f32[1024,1024]{0,1:T(8,128)} %get-tuple-element.427) | copy-start | bytes 12582916 | tf_op jit(solution)/shard_map/while
  453.8 12.1 %copy-start.7 = (f32[1024,1024]{0,1:T(8,128)S(1)}, f32[1024,1024]{0,1:T(8,128)}, u32[]{:S(2)}) copy-start(f32[1024,1024]{0,1:T(8,128)} %get-tuple-element.427) | copy-start | bytes 12582916 | tf_op jit(solution)/shard_map/while
  482.9 12.1 %copy-start.7 = (f32[1024,1024]{0,1:T(8,128)S(1)}, f32[1024,1024]{0,1:T(8,128)}, u32[]{:S(2)}) copy-start(f32[1024,1024]{0,1:T(8,128)} %get-tuple-element.427) | copy-start | bytes 12582916 | tf_op jit(solution)/shard_map/while
  512.0 12.1 %copy-start.7 = (f32[1024,1024]{0,1:T(8,128)S(1)}, f32[1024,1024]{0,1:T(8,128)}, u32[]{:S(2)}) copy-start(f32[1024,1024]{0,1:T(8,128)} %get-tuple-element.427) | copy-start | bytes 12582916 | tf_op jit(solution)/shard_map/while
  541.1 12.1 %copy-start.7 = (f32[1024,1024]{0,1:T(8,128)S(1)}, f32[1024,1024]{0,1:T(8,128)}, u32[]{:S(2)}) copy-start(f32[1024,1024]{0,1:T(8,128)} %get-tuple-element.427) | copy-start | bytes 12582916 | tf_op jit(solution)/shard_map/while
  570.2 12.1 %copy-start.7 = (f32[1024,1024]{0,1:T(8,128)S(1)}, f32[1024,1024]{0,1:T(8,128)}, u32[]{:S(2)}) copy-start(f32[1024,1024]{0,1:T(8,128)} %get-tuple-element.427) | copy-start | bytes 12582916 | tf_op jit(solution)/shard_map/while
  599.3 12.1 %copy-start.7 = (f32[1024,1024]{0,1:T(8,128)S(1)}, f32[1024,1024]{0,1:T(8,128)}, u32[]{:S(2)}) copy-start(f32[1024,1024]{0,1:T(8,128)} %get-tuple-element.427) | copy-start | bytes 12582916 | tf_op jit(solution)/shard_map/while
  628.4 12.1 %copy-start.7 = (f32[1024,1024]{0,1:T(8,128)S(1)}, f32[1024,1024]{0,1:T(8,128)}, u32[]{:S(2)}) copy-start(f32[1024,1024]{0,1:T(8,128)} %get-tuple-element.427) | copy-start | bytes 12582916 | tf_op jit(solution)/shard_map/while
  657.5 12.1 %copy-start.7 = (f32[1024,1024]{0,1:T(8,128)S(1)}, f32[1024,1024]{0,1:T(8,128)}, u32[]{:S(2)}) copy-start(f32[1024,1024]{0,1:T(8,128)} %get-tuple-element.427) | copy-start | bytes 12582916 | tf_op jit(solution)/shard_map/while
  686.6 12.1 %copy-start.7 = (f32[1024,1024]{0,1:T(8,128)S(1)}, f32[1024,1024]{0,1:T(8,128)}, u32[]{:S(2)}) copy-start(f32[1024,1024]{0,1:T(8,128)} %get-tuple-element.427) | copy-start | bytes 12582916 | tf_op jit(solution)/shard_map/while
  715.5 26.3 %copy-start.3 = (f32[1024,1024]{0,1:T(8,128)S(1)}, f32[1024,1024]{0,1:T(8,128)}, u32[]{:S(2)}) copy-start(f32[1024,1024]{0,1:T(8,128)} %get-tuple-element.96) | copy-start | bytes 12582916
  740.2 21.2 %collective-permute-start.4 = (f32[1,16,128,64]{2,3,1,0:T(8,128)S(1)}, f32[1,16,128,64]{2,3,1,0:T(8,128)S(1)}, u32[]{:S(2)}, u32[]{:S(2)}) collective-permute-start(f32[1,16,128,64]{2,3,1,0:T(8,128)S(1)} %get-tuple-element.253), channel_id=1, source_target_pairs={{0,16},{4,20},{8,24},{12,28},{16,0},{20,4},{24,8},{28,12},{1,17},{... | collective-permute-start | bytes 1572872 | tf_op jit(solution)/shard_map/ppermute | solution.py:11
  749.5 49.4 %reduce-scatter.3.cloned.1.call-start = ((), (), s32[]{:S(2)}) async-start(), calls=%async_computation.2 | async-start | bytes 655360 | tf_op jit(solution)/shard_map/reduce_scatter | solution.py:171
  749.5 16.5 %copy-start.2 = (f32[16,1024,64]{1,2,0:T(8,128)S(1)}, f32[16,1024,64]{1,2,0:T(8,128)}, u32[]{:S(2)}) copy-start(f32[16,1024,64]{1,2,0:T(8,128)} %get-tuple-element.439) | copy-start | bytes 12582916
  761.5 11.2 %copy-start.4 = (f32[1024,1024]{0,1:T(8,128)S(1)}, f32[1024,1024]{0,1:T(8,128)}, u32[]{:S(2)}) copy-start(f32[1024,1024]{0,1:T(8,128)} %get-tuple-element.96) | copy-start | bytes 12582916
  772.8 4.3 copy-start.9
Sparse Core Ops, SparseCore 0:
  749.6 21.0 reduce-scatter.4
  777.2 21.6 reduce-scatter.2
